TPU v7x, 32 devices: a whole 2x2x4 slice. The times are simulated.
32 devices in a mesh: section: 2 (over x), expert: 4 (over z), dp: 4 (over y, core).
Axes of the slice: x: 2, y: 2, z: 4, core: 2. Of those that a mesh axis runs over, the one named last changes fastest.
Arguments:
- ends: bfloat16 [2, 8192, 768], P('section', ('expert', 'dp')), may hold values from -6 to 6
- routes: int32 [2, 8192, 1], P('section', ('expert', 'dp')), may hold values from 0 to 7; in each aligned block of 256 rows (0 to 255, 256 to 511, ..., all dimensions but the last counted through in order) at most 64 rows name the same one
- norm_gain_first: bfloat16 [2, 768], P('section', 'dp'), may hold values from 0.5 to 1.5
- norm_gain_second: bfloat16 [2, 768], P('section', 'dp'), may hold values from 0.5 to 1.5
- w_query: bfloat16 [2, 768, 768], P('section', 'dp'), may hold values from -0.21875 to 0.21875
- w_key: bfloat16 [2, 768, 768], P('section', 'dp'), may hold values from -0.21875 to 0.21875
- w_value: bfloat16 [2, 768, 768], P('section', 'dp'), may hold values from -0.21875 to 0.21875
- w_output: bfloat16 [2, 768, 768], P('section', 'dp'), may hold values from -1.75 to 1.75
- w_router: bfloat16 [2, 768, 8], P('section', 'dp'), may hold values from -0.109375 to 0.109375
- bias_table: bfloat16 [2, 32, 12], P('section', 'dp'), may hold values from -4 to 4
- expert_in: bfloat16 [2, 8, 3072, 768], P('section', 'expert', 'dp'), may hold values from -0.21875 to 0.21875
- expert_out: bfloat16 [2, 8, 3072, 768], P('section', 'expert', 'dp'), may hold values from -4 to 4
Outputs:
- boundary: float32 [2, 8192, 768], P('section', ('expert', 'dp'))
- grad_gain_first: float32 [2, 768], P('section', 'dp')
- grad_gain_second: float32 [2, 768], P('section', 'dp')
- grad_query: float32 [2, 768, 768], P('section', 'dp')
- grad_key: float32 [2, 768, 768], P('section', 'dp')
- grad_value: float32 [2, 768, 768], P('section', 'dp')
- grad_output: float32 [2, 768, 768], P('section', 'dp')
- grad_router: float32 [2, 768, 8], P('section', 'dp')
- grad_table: float32 [2, 32, 12], P('section', 'dp')
- grad_expert_in: float32 [2, 8, 3072, 768], P('section', 'expert', 'dp')
- grad_expert_out: float32 [2, 8, 3072, 768], P('section', 'expert', 'dp')
Inputs may be any that keep to these rules, and one draw needn't show every extreme that they name: `routes`: within each layer, among the 256 tokens of one sequence (aligned blocks of 256 rows) no expert is named more than 64 times, a bound that some block reaches.
All inputs are finite; a program needn't handle non-finite values.
Results may differ from a plain program's by a relative error of at most 0.03.
Values may be sent and summed in bfloat16 or wider, within the bound.
A program may use at most 256 MiB of HBM per device.

v0:
```python
import jax
import jax.numpy as jnp
from jax import lax
from jax.sharding import PartitionSpec as P

SEQ = 256
MICRO = 2


EPSILON = 1e-06
PRECISE = lax.Precision.HIGHEST
LIMITS = (1, 2, 3, 4, 5, 6, 7, 8, 12, 16, 23, 32, 46, 64, 91)


def from_behind(block, axis, distance):
    devices = range(lax.axis_size(axis))
    route = [(i - distance, i) for i in devices if i - distance in devices]
    return lax.ppermute(block, axis, route)


def bucket_onehot(length, buckets):
    offsets = jnp.arange(2 * length - 1, dtype=jnp.int32) - (length - 1)
    distance = jnp.abs(offsets)
    bucket = jnp.where(offsets < 0, buckets // 2, 0).astype(jnp.int32)
    for threshold in LIMITS:
        bucket = bucket + (distance >= threshold).astype(jnp.int32)
    return (bucket[:, None] == jnp.arange(buckets, dtype=jnp.int32)[None, :]).astype(jnp.float32)


def sliding(diagonal_values, length):
    head_count, span_width = diagonal_values.shape
    tiled = jnp.broadcast_to(diagonal_values[:, None, :], (head_count, length, span_width))
    tiled = jnp.pad(tiled.reshape(head_count, length * span_width), ((0, 0), (0, length)))
    return tiled.reshape(head_count, length, span_width + 1)[:, :, :length]


def toeplitz(diagonal_values, length):
    return sliding(diagonal_values[:, ::-1], length)[:, ::-1, :]


def diagonal_sums(grid_values, length):
    head_count = grid_values.shape[0]
    span_width = 2 * length - 1
    padded = jnp.pad(grid_values[:, ::-1, :], ((0, 0), (0, 0), (0, span_width + 1 - length)))
    flattened = padded.reshape(head_count, length * (span_width + 1))[:, : length * span_width]
    return jnp.sum(flattened.reshape(head_count, length, span_width), axis=1)[:, ::-1]


def root_scale(values):
    return lax.rsqrt(jnp.mean(values * values, axis=-1, keepdims=True) + EPSILON)


def norm_backward(grad_normed, values, factor, gain_value):
    scaled = grad_normed * gain_value
    grad_gain = jnp.sum(grad_normed * values * factor, axis=0)
    grad_values = factor * scaled - values * factor * factor * factor * jnp.mean(
        scaled * values, axis=-1, keepdims=True
    )
    return (grad_values, grad_gain)


def expert_forward(grouped, w_in_use, w_out_use):
    before = jnp.einsum("necd,efd->necf", grouped, w_in_use, preferred_element_type=jnp.float32)
    activated = jax.nn.gelu(before).astype(jnp.bfloat16)
    produced = jnp.einsum(
        "necf,efd->necd", activated, w_out_use, preferred_element_type=jnp.float32
    )
    return (produced.astype(jnp.bfloat16), (grouped, before))


def expert_backward(grad_rows, kept_rows, w_in_use, w_out_use):
    inputs_all, before = kept_rows
    activated = jax.nn.gelu(before).astype(jnp.bfloat16)
    grad_w_out = jnp.einsum(
        "necf,necd->efd", activated, grad_rows, preferred_element_type=jnp.float32
    )
    grad_activated = jnp.einsum(
        "necd,efd->necf", grad_rows, w_out_use, preferred_element_type=jnp.float32
    )
    grad_before = jax.vjp(jax.nn.gelu, before)[1](grad_activated)[0].astype(jnp.bfloat16)
    grad_w_in = jnp.einsum(
        "necf,necd->efd", grad_before, inputs_all, preferred_element_type=jnp.float32
    )
    grad_inputs = jnp.einsum(
        "necf,efd->necd", grad_before, w_in_use, preferred_element_type=jnp.float32
    )
    return (grad_inputs.astype(jnp.bfloat16), grad_w_in, grad_w_out)


def layer_forward(arriving, target_expert, mixer_set, position_bias, w_in_use, w_out_use):
    gain_first, gain_second, w_query, w_key, w_value, w_output, w_router = mixer_set
    hidden = arriving.astype(jnp.float32)
    length, model_width = hidden.shape
    head_count = position_bias.shape[0]
    head_size = model_width // head_count
    head_shape = (length, head_count, head_size)
    factor = head_size ** (-0.5)
    first_scale = root_scale(hidden)
    normed = (hidden * first_scale * gain_first.astype(jnp.float32)).astype(jnp.bfloat16)
    queries = jnp.dot(normed, w_query, preferred_element_type=jnp.float32).astype(jnp.bfloat16)
    key_rows = jnp.dot(normed, w_key, preferred_element_type=jnp.float32).astype(jnp.bfloat16)
    value_rows = jnp.dot(normed, w_value, preferred_element_type=jnp.float32).astype(jnp.bfloat16)
    scores = (
        jnp.einsum(
            "qhd,khd->hqk",
            queries.reshape(head_shape),
            key_rows.reshape(head_shape),
            preferred_element_type=jnp.float32,
        )
        * factor
        + position_bias
    )
    row_peak = jnp.max(scores, axis=-1, keepdims=True)
    log_total = row_peak + jnp.log(jnp.sum(jnp.exp(scores - row_peak), axis=-1, keepdims=True))
    shares = jnp.exp(scores - log_total).astype(jnp.bfloat16)
    attended = jnp.einsum(
        "hqk,khd->qhd", shares, value_rows.reshape(head_shape), preferred_element_type=jnp.float32
    )
    attended = attended.reshape(length, model_width).astype(jnp.bfloat16)
    mixed = hidden + jnp.dot(attended, w_output, preferred_element_type=jnp.float32)
    second_scale = root_scale(mixed)
    routed = (mixed * second_scale * gain_second.astype(jnp.float32)).astype(jnp.bfloat16)
    logits = jnp.dot(routed, w_router, preferred_element_type=jnp.float32)
    router = jax.nn.softmax(logits, axis=-1)
    experts = w_router.shape[1]
    capacity = max(2, 2 * length // experts)
    chosen = target_expert[:, None] == jnp.arange(experts, dtype=jnp.int32)[None, :]
    gate_value = jnp.sum(jnp.where(chosen, router, 0.0), axis=-1)
    counts = jnp.cumsum(chosen.astype(jnp.int32), axis=0)
    slot_rank = jnp.sum(jnp.where(chosen, counts, 0), axis=-1) - 1
    slot_index = target_expert * capacity + slot_rank
    outgoing = jnp.zeros((experts * capacity, model_width), jnp.bfloat16).at[slot_index].set(routed)
    received = lax.all_to_all(
        outgoing.reshape(experts, capacity, model_width),
        "expert",
        split_axis=0,
        concat_axis=0,
        tiled=True,
    )
    local_experts = w_in_use.shape[0]
    grouped = received.reshape(experts // local_experts, local_experts, capacity, model_width)
    produced, kept_rows = expert_forward(grouped, w_in_use, w_out_use)
    returned = lax.all_to_all(
        produced.reshape(experts, capacity, model_width),
        "expert",
        split_axis=0,
        concat_axis=0,
        tiled=True,
    )
    fetched = returned.reshape(experts * capacity, model_width)[slot_index].astype(jnp.float32)
    result = mixed + gate_value[:, None] * fetched
    stored = (
        hidden,
        normed,
        first_scale,
        queries,
        key_rows,
        value_rows,
        log_total,
        attended,
        mixed,
        second_scale,
        routed,
        router,
        chosen,
        gate_value,
        slot_index,
        fetched,
        kept_rows,
    )
    return (result, stored)


def layer_backward(grad_out, stored, mixer_set, position_bias, w_in_use, w_out_use):
    gain_first, gain_second, w_query, w_key, w_value, w_output, w_router = mixer_set
    (
        hidden,
        normed,
        first_scale,
        queries,
        key_rows,
        value_rows,
        log_total,
        attended,
        mixed,
        second_scale,
        routed,
        router,
        chosen,
        gate_value,
        slot_index,
        fetched,
        kept_rows,
    ) = stored
    length, model_width = hidden.shape
    head_count = position_bias.shape[0]
    head_size = model_width // head_count
    head_shape = (length, head_count, head_size)
    factor = head_size ** (-0.5)
    experts = w_router.shape[1]
    capacity = max(2, 2 * length // experts)
    local_experts = w_in_use.shape[0]
    grad_gate = jnp.sum(grad_out * fetched, axis=-1)
    grad_fetched = (gate_value[:, None] * grad_out).astype(jnp.bfloat16)
    grad_outgoing = (
        jnp.zeros((experts * capacity, model_width), jnp.bfloat16).at[slot_index].set(grad_fetched)
    )
    grad_received = lax.all_to_all(
        grad_outgoing.reshape(experts, capacity, model_width),
        "expert",
        split_axis=0,
        concat_axis=0,
        tiled=True,
    )
    grad_grouped = grad_received.reshape(
        experts // local_experts, local_experts, capacity, model_width
    )
    grad_inputs, grad_w_in, grad_w_out = expert_backward(
        grad_grouped, kept_rows, w_in_use, w_out_use
    )
    grad_returned = lax.all_to_all(
        grad_inputs.reshape(experts, capacity, model_width),
        "expert",
        split_axis=0,
        concat_axis=0,
        tiled=True,
    )
    grad_routed = grad_returned.reshape(experts * capacity, model_width)[slot_index].astype(
        jnp.float32
    )
    grad_logits = (
        (gate_value * grad_gate)[:, None] * (chosen.astype(jnp.float32) - router)
    ).astype(jnp.bfloat16)
    grad_routed = grad_routed + jnp.einsum(
        "se,de->sd", grad_logits, w_router, preferred_element_type=jnp.float32
    )
    grad_router = jnp.einsum("sd,se->de", routed, grad_logits, preferred_element_type=jnp.float32)
    norm_grad, grad_gain_second = norm_backward(
        grad_routed, mixed, second_scale, gain_second.astype(jnp.float32)
    )
    grad_mixed = grad_out + norm_grad
    grad_branch = grad_mixed.astype(jnp.bfloat16)
    grad_output = jnp.einsum("sd,se->de", attended, grad_branch, preferred_element_type=jnp.float32)
    grad_attended = jnp.einsum(
        "se,de->sd", grad_branch, w_output, preferred_element_type=jnp.float32
    )
    grad_attended = grad_attended.astype(jnp.bfloat16).reshape(head_shape)
    query_heads = queries.reshape(head_shape)
    key_heads = key_rows.reshape(head_shape)
    scores = (
        jnp.einsum("qhd,khd->hqk", query_heads, key_heads, preferred_element_type=jnp.float32)
        * factor
        + position_bias
    )
    softmax_rows = jnp.exp(scores - log_total)
    shares = softmax_rows.astype(jnp.bfloat16)
    grad_values = jnp.einsum(
        "hqk,qhd->khd", shares, grad_attended, preferred_element_type=jnp.float32
    )
    grad_values = grad_values.astype(jnp.bfloat16).reshape(length, model_width)
    grad_shares = jnp.einsum(
        "qhd,khd->hqk",
        grad_attended,
        value_rows.reshape(head_shape),
        preferred_element_type=jnp.float32,
    )
    grad_scores = softmax_rows * (
        grad_shares - jnp.sum(grad_shares * softmax_rows, axis=-1, keepdims=True)
    )
    grad_scores = grad_scores.astype(jnp.bfloat16)
    grad_diagonal = diagonal_sums(grad_scores.astype(jnp.float32), length)
    grad_queries = (
        jnp.einsum("hqk,khd->qhd", grad_scores, key_heads, preferred_element_type=jnp.float32)
        * factor
    )
    grad_queries = grad_queries.astype(jnp.bfloat16).reshape(length, model_width)
    grad_keys = (
        jnp.einsum("hqk,qhd->khd", grad_scores, query_heads, preferred_element_type=jnp.float32)
        * factor
    )
    grad_keys = grad_keys.astype(jnp.bfloat16).reshape(length, model_width)
    grad_query = jnp.einsum("sd,se->de", normed, grad_queries, preferred_element_type=jnp.float32)
    grad_key = jnp.einsum("sd,se->de", normed, grad_keys, preferred_element_type=jnp.float32)
    grad_value = jnp.einsum("sd,se->de", normed, grad_values, preferred_element_type=jnp.float32)
    grad_normed = jnp.einsum("se,de->sd", grad_queries, w_query, preferred_element_type=jnp.float32)
    grad_normed = grad_normed + jnp.einsum(
        "se,de->sd", grad_keys, w_key, preferred_element_type=jnp.float32
    )
    grad_normed = grad_normed + jnp.einsum(
        "se,de->sd", grad_values, w_value, preferred_element_type=jnp.float32
    )
    first_grad, grad_gain_first = norm_backward(
        grad_normed, hidden, first_scale, gain_first.astype(jnp.float32)
    )
    grad_hidden = grad_mixed + first_grad
    mixer_grads = (
        grad_gain_first,
        grad_gain_second,
        grad_query,
        grad_key,
        grad_value,
        grad_output,
        grad_router,
        grad_diagonal,
    )
    return (grad_hidden, mixer_grads, (grad_w_in, grad_w_out))


def reduce_mixer(mixer_grads, onehot_rows):
    gain_a, gain_b, grad_query, grad_key, grad_value, grad_output, grad_router, grad_diagonal = (
        mixer_grads
    )
    grad_table = jnp.einsum("wb,hw->bh", onehot_rows, grad_diagonal, precision=PRECISE)
    shards = (
        lax.psum_scatter(gain_a.astype(jnp.bfloat16), "dp", scatter_dimension=0, tiled=True).astype(
            jnp.float32
        ),
        lax.psum_scatter(gain_b.astype(jnp.bfloat16), "dp", scatter_dimension=0, tiled=True).astype(
            jnp.float32
        ),
        lax.psum_scatter(
            grad_query.astype(jnp.bfloat16), "dp", scatter_dimension=0, tiled=True
        ).astype(jnp.float32),
        lax.psum_scatter(
            grad_key.astype(jnp.bfloat16), "dp", scatter_dimension=0, tiled=True
        ).astype(jnp.float32),
        lax.psum_scatter(
            grad_value.astype(jnp.bfloat16), "dp", scatter_dimension=0, tiled=True
        ).astype(jnp.float32),
        lax.psum_scatter(
            grad_output.astype(jnp.bfloat16), "dp", scatter_dimension=0, tiled=True
        ).astype(jnp.float32),
        lax.psum_scatter(
            grad_router.astype(jnp.bfloat16), "dp", scatter_dimension=0, tiled=True
        ).astype(jnp.float32),
        lax.psum_scatter(
            grad_table.astype(jnp.bfloat16), "dp", scatter_dimension=0, tiled=True
        ).astype(jnp.float32),
    )
    return (
        lax.psum(shards[0].astype(jnp.bfloat16), "expert").astype(jnp.float32),
        lax.psum(shards[1].astype(jnp.bfloat16), "expert").astype(jnp.float32),
        lax.psum(shards[2].astype(jnp.bfloat16), "expert").astype(jnp.float32),
        lax.psum(shards[3].astype(jnp.bfloat16), "expert").astype(jnp.float32),
        lax.psum(shards[4].astype(jnp.bfloat16), "expert").astype(jnp.float32),
        lax.psum(shards[5].astype(jnp.bfloat16), "expert").astype(jnp.float32),
        lax.psum(shards[6].astype(jnp.bfloat16), "expert").astype(jnp.float32),
        lax.psum(shards[7].astype(jnp.bfloat16), "expert").astype(jnp.float32),
    )


def reduce_experts(expert_grads):
    return (
        lax.psum_scatter(
            expert_grads[0].astype(jnp.bfloat16), "dp", scatter_dimension=1, tiled=True
        ).astype(jnp.float32),
        lax.psum_scatter(
            expert_grads[1].astype(jnp.bfloat16), "dp", scatter_dimension=1, tiled=True
        ).astype(jnp.float32),
    )


def add_trees(running, addition):
    if running is None:
        return addition
    return jax.tree.map(jnp.add, running, addition)


def local(
    ends,
    routes,
    norm_gain_first,
    norm_gain_second,
    w_query,
    w_key,
    w_value,
    w_output,
    w_router,
    bias_table,
    expert_in,
    expert_out,
):
    is_first = lax.axis_index("section") == 0
    gathered = (
        lax.all_gather(norm_gain_first, "dp", axis=1, tiled=True),
        lax.all_gather(norm_gain_second, "dp", axis=1, tiled=True),
        lax.all_gather(w_query, "dp", axis=1, tiled=True),
        lax.all_gather(w_key, "dp", axis=1, tiled=True),
        lax.all_gather(w_value, "dp", axis=1, tiled=True),
        lax.all_gather(w_output, "dp", axis=1, tiled=True),
        lax.all_gather(w_router, "dp", axis=1, tiled=True),
        lax.all_gather(bias_table, "dp", axis=1, tiled=True),
    )
    mixer_full = tuple((member[0] for member in gathered))
    mixer_set = mixer_full[:7]
    bias_rows = mixer_full[7].astype(jnp.float32)
    expert_full = (
        lax.all_gather(expert_in, "dp", axis=2, tiled=True),
        lax.all_gather(expert_out, "dp", axis=2, tiled=True),
    )
    w_in_use = expert_full[0][0]
    w_out_use = expert_full[1][0]
    model_width = ends.shape[2]
    onehot_rows = bucket_onehot(SEQ, bias_rows.shape[0])
    diagonal_values = jnp.einsum("wb,bh->hw", onehot_rows, bias_rows, precision=PRECISE)
    position_bias = toeplitz(diagonal_values, SEQ)
    local_rows = ends[0]
    local_routes = routes[0, :, 0]

    def block_rows(source, micro_index):
        return source[micro_index * SEQ : (micro_index + 1) * SEQ]

    stored_list = []
    results = []
    arriving = jnp.zeros((SEQ, model_width), jnp.bfloat16)
    for tick_number in range(MICRO + 1):
        own_micro = min(tick_number, MICRO - 1)
        prior_micro = max(tick_number - 1, 0)
        layer_input = jnp.where(is_first, block_rows(local_rows, own_micro), arriving)
        target_expert = jnp.where(
            is_first, block_rows(local_routes, own_micro), block_rows(local_routes, prior_micro)
        )
        result, stored = layer_forward(
            layer_input, target_expert, mixer_set, position_bias, w_in_use, w_out_use
        )
        stored_list.append(stored)
        results.append(result)
        if tick_number < MICRO:
            arriving = from_behind(result.astype(jnp.bfloat16), "section", 1)
    input_grads = [None] * MICRO
    returning = jnp.zeros((SEQ, model_width), jnp.bfloat16)
    mixer_sum = None
    expert_sum = None
    for step_number in range(MICRO + 1):
        if step_number < MICRO:
            cotangent = block_rows(local_rows, MICRO - 1 - step_number).astype(jnp.float32)
        else:
            cotangent = jnp.zeros((SEQ, model_width), jnp.float32)
        grad_out = jnp.where(is_first, returning.astype(jnp.float32), cotangent)
        grad_hidden, mixer_grads, expert_grads = layer_backward(
            grad_out,
            stored_list[MICRO - step_number],
            mixer_set,
            position_bias,
            w_in_use,
            w_out_use,
        )
        if step_number < MICRO:
            returning = from_behind(grad_hidden.astype(jnp.bfloat16), "section", -1)
        if step_number >= 1:
            input_grads[MICRO - step_number] = grad_hidden
        mixer_sum = add_trees(mixer_sum, mixer_grads)
        expert_sum = add_trees(expert_sum, expert_grads)
    mixer_sum = reduce_mixer(mixer_sum, onehot_rows)
    expert_sum = reduce_experts(expert_sum)
    pieces = [
        jnp.where(is_first, input_grads[micro_index], results[micro_index + 1])
        for micro_index in range(MICRO)
    ]
    boundary = jnp.concatenate(pieces, axis=0)[None]
    return (
        boundary,
        mixer_sum[0][None],
        mixer_sum[1][None],
        mixer_sum[2][None],
        mixer_sum[3][None],
        mixer_sum[4][None],
        mixer_sum[5][None],
        mixer_sum[6][None],
        mixer_sum[7][None],
        expert_sum[0][None],
        expert_sum[1][None],
    )


def solution(mesh):
    in_specs = (
        P("section", ("expert", "dp"), None),
        P("section", ("expert", "dp"), None),
        P("section", "dp"),
        P("section", "dp"),
        P("section", "dp", None),
        P("section", "dp", None),
        P("section", "dp", None),
        P("section", "dp", None),
        P("section", "dp", None),
        P("section", "dp", None),
        P("section", "expert", "dp", None),
        P("section", "expert", "dp", None),
    )
    out_specs = (
        P("section", ("expert", "dp"), None),
        P("section", "dp"),
        P("section", "dp"),
        P("section", "dp", None),
        P("section", "dp", None),
        P("section", "dp", None),
        P("section", "dp", None),
        P("section", "dp", None),
        P("section", "dp", None),
        P("section", "expert", "dp", None),
        P("section", "expert", "dp", None),
    )
    return jax.shard_map(local, mesh=mesh, in_specs=in_specs, out_specs=out_specs, check_vma=False)
```

profile of v0, /device:TPU:0, one launch (start us, length us, event | category | flops | bytes accessed | tf_op | source)
XLA Modules:
  0.0 1073.8 jit_solution(242019794249780462)
XLA Ops:
  50.9 22.4 %rev.25 = f32[12,256,256]{1,2,0:T(8,128)S(1)} reverse(f32[12,256,256]{1,2,0:T(8,128)} %copy.222), dimensions={1} | reverse | bytes 6291456 | tf_op jit(solution)/shard_map/rev | solution.py:38
  98.1 25.3 %all_to_all.60 = bf16[8,64,768]{2,1,0:T(8,128)(2,1)S(1)} all-to-all(bf16[8,64,768]{2,1,0:T(8,128)(2,1)S(1)} %bitcast.620), channel_id=1, replica_groups=mesh['section'=2,'expert'=4,'dp'=4] {'expert'}, dimensions={0} | all-to-all | bytes 1572864 | tf_op jit(solution)/shard_map/all_to_all | solution.py:133
  123.3 29.2 %all-gather.15.cloned.1.call-done = bf16[1,2,3072,768]{3,2,1,0:T(8,128)(2,1)} async-done(((bf16[1,2,768,768]{3,2,1,0:T(8,128)(2,1)}), bf16[1,2,3072,768]{3,2,1,0:T(8,128)(2,1)}) %all-gather.15.cloned.1.call-update) | async-done | bytes 9437200 | tf_op jit(solution)/shard_map/all_gather | solution.py:398
  152.6 11.5 %fusion.24 = f32[2,4,64,3072]{3,2,1,0:T(8,128)} fusion(bf16[1,2,3072,768]{3,2,1,0:T(8,128)(2,1)} %all-gather.15.cloned.1.call-done, bf16[4,2,64,768]{3,2,1,0:T(8,128)(2,1)S(1)} %bitcast.563), kind=kOutput, calls=%fused_computation.40 | convolution fusion | flops 2415919104 | bytes 16515072 | tf_op jit(solution)/shard_map/necd,efd->necf/dot_general | solution.py:63
  164.1 54.2 %all-gather.17.cloned.1.call-done = bf16[1,2,3072,768]{3,2,1,0:T(8,128)(2,1)} async-done(((bf16[1,2,768,768]{3,2,1,0:T(8,128)(2,1)}), bf16[1,2,3072,768]{3,2,1,0:T(8,128)(2,1)}) %all-gather.17.cloned.1.call-update) | async-done | bytes 9437200 | tf_op jit(solution)/shard_map/all_gather | solution.py:399
  239.9 13.0 %all-to-all-done.1 = bf16[8,64,768]{2,1,0:T(8,128)(2,1)S(1)} async-done(((bf16[8,64,768]{2,1,0:T(8,128)(2,1)}), bf16[8,64,768]{2,1,0:T(8,128)(2,1)S(1)}, u32[]{:S(2)}, u32[]{:S(2)}) %all-to-all-start.1) | async-done | bytes 786464 | tf_op jit(solution)/shard_map/all_to_all | solution.py:143
  280.7 22.2 %all_to_all.61 = bf16[8,64,768]{2,1,0:T(8,128)(2,1)S(1)} all-to-all(bf16[8,64,768]{2,1,0:T(8,128)(2,1)} %bitcast.621), channel_id=1, replica_groups=mesh['section'=2,'expert'=4,'dp'=4] {'expert'}, dimensions={0} | all-to-all | bytes 1572864 | tf_op jit(solution)/shard_map/all_to_all | solution.py:133
  326.3 15.5 %all-to-all-done.3 = bf16[8,64,768]{2,1,0:T(8,128)(2,1)} async-done(((bf16[8,64,768]{2,1,0:T(8,128)(2,1)}), bf16[8,64,768]{2,1,0:T(8,128)(2,1)}, u32[]{:S(2)}, u32[]{:S(2)}) %all-to-all-start.3) | async-done | bytes 786464 | tf_op jit(solution)/shard_map/all_to_all | solution.py:143
  396.3 10.2 all-to-all-done.5
  466.0 12.3 %all-to-all-done.6 = bf16[8,64,768]{2,1,0:T(8,128)(2,1)} async-done(((bf16[8,64,768]{2,1,0:T(8,128)(2,1)}), bf16[8,64,768]{2,1,0:T(8,128)(2,1)}, u32[]{:S(2)}, u32[]{:S(2)}) %all-to-all-start.6) | async-done | bytes 786464 | tf_op jit(solution)/shard_map/all_to_all | solution.py:221
  500.5 10.9 %collective-permute-done.2 = bf16[256,768]{1,0:T(8,128)(2,1)} collective-permute-done((bf16[256,768]{1,0:T(8,128)(2,1)S(1)}, bf16[256,768]{1,0:T(8,128)(2,1)}, u32[]{:S(2)}, u32[]{:S(2)}) %collective-permute-start.2) | collective-permute-done | bytes 393248 | tf_op jit(solution)/shard_map/ppermute | solution.py:18
  514.7 22.7 %all_to_all.62 = bf16[8,64,768]{2,1,0:T(8,128)(2,1)S(1)} all-to-all(bf16[8,64,768]{2,1,0:T(8,128)(2,1)} %bitcast.619), channel_id=1, replica_groups=mesh['section'=2,'expert'=4,'dp'=4] {'expert'}, dimensions={0} | all-to-all | bytes 1572864 | tf_op jit(solution)/shard_map/all_to_all | solution.py:208
  537.3 12.2 %fusion.39 = bf16[4,2,64,3072]{3,2,0,1:T(8,128)(2,1)S(1)} fusion(f32[2,4,64,3072]{3,2,1,0:T(8,128)} %copy-done.50, bf16[1,2,3072,768]{3,2,1,0:T(8,128)(2,1)} %all-gather.17.cloned.1.call-done, bf16[4,2,64,768]{3,2,1,0:T(8,128)(2,1)S(1)} %bitcast.628), kind=kOutput, calls=%fused_computation.61 | convolution fusion | flops 2447376384 | bytes 19660800 | tf_op jit(solution)/shard_map/necd,efd->necf/dot_general | solution.py:77
  564.9 16.4 %all-to-all-done.9 = bf16[8,64,768]{2,1,0:T(8,128)(2,1)} async-done(((bf16[8,64,768]{2,1,0:T(8,128)(2,1)}), bf16[8,64,768]{2,1,0:T(8,128)(2,1)}, u32[]{:S(2)}, u32[]{:S(2)}) %all-to-all-start.9) | async-done | bytes 786464 | tf_op jit(solution)/shard_map/all_to_all | solution.py:221
  603.6 10.7 collective-permute-done.3
  616.3 21.3 %all_to_all.63 = bf16[8,64,768]{2,1,0:T(8,128)(2,1)S(1)} all-to-all(bf16[8,64,768]{2,1,0:T(8,128)(2,1)S(1)} %bitcast.618), channel_id=1, replica_groups=mesh['section'=2,'expert'=4,'dp'=4] {'expert'}, dimensions={0} | all-to-all | bytes 1572864 | tf_op jit(solution)/shard_map/all_to_all | solution.py:208
  637.6 12.2 %fusion.32 = bf16[4,2,64,3072]{3,2,0,1:T(8,128)(2,1)S(1)} fusion(f32[2,4,64,3072]{3,2,1,0:T(8,128)} %fusion.24, bf16[1,2,3072,768]{3,2,1,0:T(8,128)(2,1)} %all-gather.17.cloned.1.call-done, bf16[4,2,64,768]{3,2,1,0:T(8,128)(2,1)S(1)} %bitcast.622), kind=kOutput, calls=%fused_computation.54 | convolution fusion | flops 2447376384 | bytes 19660800 | tf_op jit(solution)/shard_map/necd,efd->necf/dot_general | solution.py:77
  662.1 13.8 %all-to-all-done.11 = bf16[8,64,768]{2,1,0:T(8,128)(2,1)S(1)} async-done(((bf16[8,64,768]{2,1,0:T(8,128)(2,1)}), bf16[8,64,768]{2,1,0:T(8,128)(2,1)S(1)}, u32[]{:S(2)}, u32[]{:S(2)}) %all-to-all-start.11) | async-done | bytes 786464 | tf_op jit(solution)/shard_map/all_to_all | solution.py:221
  708.2 11.3 %fusion.190 = f32[2,3072,768,1]{2,1,3,0:T(8,128)} fusion(bf16[4,2,64,3072]{3,2,0,1:T(8,128)(2,1)} %copy-done.189, bf16[4,2,64,768]{3,2,1,0:T(8,128)(2,1)} %bitcast.69), kind=kOutput, calls=%fused_computation.290 | convolution fusion | flops 2415919104 | bytes 22806528 | tf_op jit(solution)/shard_map/necf,necd->efd/dot_general | solution.py:81
  721.1 11.1 %fusion.196 = f32[2,3072,768,1]{2,1,3,0:T(8,128)} fusion(bf16[4,2,64,3072]{3,2,0,1:T(8,128)(2,1)} %copy-done.190, bf16[4,2,64,768]{3,2,1,0:T(8,128)(2,1)S(1)} %bitcast.610), kind=kOutput, calls=%fused_computation.296 | convolution fusion | flops 2415919104 | bytes 22806528 | tf_op jit(solution)/shard_map/necf,necd->efd/dot_general | solution.py:81
  732.2 11.2 %reduce-scatter.12.cloned.1.call-done = bf16[192,768]{1,0:T(8,128)(2,1)} async-done(((bf16[768,768]{1,0:T(8,128)(2,1)}), bf16[192,768]{1,0:T(8,128)(2,1)}) %reduce-scatter.12.cloned.1.call-update) | async-done | bytes 294928 | tf_op jit(solution)/shard_map/reduce_scatter | solution.py:324
  743.4 28.3 %reduce-scatter.14.cloned.1.call-done = bf16[192,768]{1,0:T(8,128)(2,1)} async-done(((bf16[768,768]{1,0:T(8,128)(2,1)}), bf16[192,768]{1,0:T(8,128)(2,1)}) %reduce-scatter.14.cloned.1.call-update) | async-done | bytes 294928 | tf_op jit(solution)/shard_map/reduce_scatter | solution.py:327
  771.7 28.4 %reduce-scatter.16.cloned.1.call-done = bf16[192,768]{1,0:T(8,128)(2,1)} async-done(((bf16[768,768]{1,0:T(8,128)(2,1)}), bf16[192,768]{1,0:T(8,128)(2,1)}) %reduce-scatter.16.cloned.1.call-update) | async-done | bytes 294928 | tf_op jit(solution)/shard_map/reduce_scatter | solution.py:330
  800.6 18.6 %fusion.1 = bf16[2,3072,768]{2,1,0:T(8,128)(2,1)} fusion(f32[2,3072,768,1]{2,1,3,0:T(8,128)} %fusion.196, f32[2,3072,768,1]{2,1,3,0:T(8,128)} %fusion.190, bf16[4,2,64,3072]{3,2,0,1:T(8,128)(2,1)} %copy-done.98, bf16[4,2,64,768]{3,2,1,0:T(8,128)(2,1)S(1)} %bitcast.564), kind=kOutput, calls=%fused_computation.16 | convolution fusion | flops 2430074880 | bytes 51118080 | tf_op jit(solution)/shard_map/necf,necd->efd/dot_general | solution.py:81
  819.3 12.8 %fusion.193 = f32[2,3072,768,1]{2,1,3,0:T(8,128)} fusion(bf16[4,2,64,768]{3,2,1,0:T(8,128)(2,1)} %bitcast.66, f32[2,4,64,3072]{3,2,1,0:T(8,128)} %copy-done.51), kind=kOutput, calls=%fused_computation.293 | convolution fusion | flops 2430074880 | bytes 25952256 | tf_op jit(solution)/shard_map/necf,necd->efd/dot_general | solution.py:74
  832.1 12.7 %fusion.187 = f32[2,3072,768,1]{2,1,3,0:T(8,128)} fusion(bf16[4,2,64,768]{3,2,1,0:T(8,128)(2,1)S(1)} %bitcast.629, f32[2,4,64,3072]{3,2,1,0:T(8,128)} %copy-done.50), kind=kOutput, calls=%fused_computation.287 | convolution fusion | flops 2430074880 | bytes 25952256 | tf_op jit(solution)/shard_map/necf,necd->efd/dot_general | solution.py:74
  844.7 19.6 %fusion = bf16[2,3072,768]{2,1,0:T(8,128)(2,1)} fusion(f32[2,3072,768,1]{2,1,3,0:T(8,128)} %fusion.187, f32[2,3072,768,1]{2,1,3,0:T(8,128)} %fusion.193, bf16[4,2,64,768]{3,2,1,0:T(8,128)(2,1)S(1)} %bitcast.623, f32[2,4,64,3072]{3,2,1,0:T(8,128)} %fusion.24), kind=kOutput, calls=%fused_computation.13 | convolution fusion | flops 2444230656 | bytes 54263808 | tf_op jit(solution)/shard_map/necf,necd->efd/dot_general | solution.py:74
  865.7 17.2 %rev.26 = f32[12,256,256]{1,2,0:T(8,128)} reverse(bf16[12,256,256]{1,2,0:T(8,128)(2,1)S(1)} %copy-done.18), dimensions={1} | reverse | bytes 4718592 | tf_op jit(solution)/shard_map/rev | solution.py:44
  913.2 17.2 %rev.28 = f32[12,256,256]{1,2,0:T(8,128)} reverse(bf16[12,256,256]{1,2,0:T(8,128)(2,1)S(1)} %copy-done.20), dimensions={1} | reverse | bytes 4718592 | tf_op jit(solution)/shard_map/rev | solution.py:44
  959.2 17.2 %rev.30 = f32[12,256,256]{1,2,0:T(8,128)} reverse(bf16[12,256,256]{1,2,0:T(8,128)(2,1)S(1)} %copy-done.23), dimensions={1} | reverse | bytes 4718592 | tf_op jit(solution)/shard_map/rev | solution.py:44
  1014.0 12.3 %all-reduce.9 = (bf16[768]{0:T(1024)(128)(2,1)}, bf16[768]{0:T(1024)(128)(2,1)}, bf16[32,12]{1,0:T(8,128)(2,1)}) all-reduce(bf16[768]{0:T(1024)(128)(2,1)} %add_convert_fusion.5, bf16[768]{0:T(1024)(128)(2,1)} %add_convert_fusion.4, ...), channel_id=2, replica_groups=mesh['section'=2,'expert'=4,'dp'=4] {'dp'}, use_global_device_ids=true, to_apply=%region_51.52.clone | all-reduce | flops 1920 | bytes 7680
  1030.2 12.7 %all-reduce.11 = (bf16[1,192]{1,0:T(2,128)(2,1)}, bf16[1,192]{1,0:T(2,128)(2,1)}, bf16[1,192,8]{1,2,0:T(8,128)(2,1)}, bf16[1,8,12]{2,1,0:T(8,128)(2,1)}) all-reduce(bf16[1,192]{1,0:T(2,128)(2,1)} %broadcast_in_dim.77, bf16[1,192]{1,0:T(2,128)(2,1)} %broadcast_in_dim.79, ...), channel_id=1, replica_groups=mesh['section'=2,'expert'=4,'dp'=4] {'expert'}, use_global_device_ids=true, to_apply=%region_52.53 | all-reduce | flops 2016 | bytes 8064 | tf_op jit(solution)/shard_map/psum | solution.py:341
  (688 shorter events, 488.4 us)
Async XLA Ops:
  7.2 71.3 %all-gather.7.cloned.1.call-start = ((), (), s32[]{:S(2)}) async-start(), calls=%async_computation.19 | async-start | bytes 1474560 | tf_op jit(solution)/shard_map/all_gather | solution.py:389
  8.0 73.4 %all-gather.9.cloned.1.call-start = ((), (), s32[]{:S(2)}) async-start(), calls=%async_computation.20 | async-start | bytes 1474560 | tf_op jit(solution)/shard_map/all_gather | solution.py:387
  8.7 76.5 %all-gather.11.cloned.1.call-start = ((), (), s32[]{:S(2)}) async-start(), calls=%async_computation.21 | async-start | bytes 1474560 | tf_op jit(solution)/shard_map/all_gather | solution.py:388
  9.4 84.5 %all-gather.13.cloned.1.call-start = ((), (), s32[]{:S(2)}) async-start(), calls=%async_computation.22 | async-start | bytes 1474560 | tf_op jit(solution)/shard_map/all_gather | solution.py:390
  10.0 142.6 %all-gather.15.cloned.1.call-start = ((), (), s32[]{:S(2)}) async-start(), calls=%async_computation.23 | async-start | bytes 11796480 | tf_op jit(solution)/shard_map/all_gather | solution.py:398
  10.6 207.7 %all-gather.17.cloned.1.call-start = ((), (), s32[]{:S(2)}) async-start(), calls=%async_computation.24 | async-start | bytes 11796480 | tf_op jit(solution)/shard_map/all_gather | solution.py:399
  21.4 680.7 %copy-start.105 = (f32[768]{0:T(1024)}, f32[768]{0:T(1024)S(1)}, u32[]{:S(2)}) copy-start(f32[768]{0:T(1024)S(1)} %mul.921) | copy-start | bytes 9220
  73.3 166.1 %copy-start.125 = (s32[1,256,1]{1,2,0:T(1,128)}, s32[1,256,1]{1,2,0:T(1,128)S(1)}, u32[]{:S(2)}) copy-start(s32[1,256,1]{1,2,0:T(1,128)S(1)} %get-tuple-element.46) | copy-start | bytes 3076
  96.1 158.0 %copy-start.24 = (f32[256,768]{1,0:T(8,128)}, f32[256,768]{1,0:T(8,128)S(1)}, u32[]{:S(2)}) copy-start(f32[256,768]{1,0:T(8,128)S(1)} %get-tuple-element.52) | copy-start | bytes 2359300
  96.1 142.8 %copy-start.149 = (f32[256]{0:T(256)}, f32[256]{0:T(256)S(1)}, u32[]{:S(2)}) copy-start(f32[256]{0:T(256)S(1)} %add_rsqrt_fusion.4) | copy-start | bytes 3076
  227.7 25.1 %all-to-all-start.1 = ((bf16[8,64,768]{2,1,0:T(8,128)(2,1)}), bf16[8,64,768]{2,1,0:T(8,128)(2,1)S(1)}, u32[]{:S(2)}, u32[]{:S(2)}) async-start(bf16[8,64,768]{2,1,0:T(8,128)(2,1)} %bitcast.33), calls=%async_computation.1 | async-start | bytes 1572864 | tf_op jit(solution)/shard_map/all_to_all | solution.py:143
  254.3 11.2 %collective-permute-start = (bf16[256,768]{1,0:T(8,128)(2,1)S(1)}, bf16[256,768]{1,0:T(8,128)(2,1)S(1)}, u32[]{:S(2)}, u32[]{:S(2)}) collective-permute-start(bf16[256,768]{1,0:T(8,128)(2,1)S(1)} %fusion.158), channel_id=1, source_target_pairs={{0,16},{1,17},{2,18},{3,19},{4,20},{5,21},{6,22},{7,23},{8,24},{9,... | collective-permute-start | bytes 1179656 | tf_op jit(solution)/shard_map/ppermute | solution.py:18
  318.6 23.2 %all-to-all-start.3 = ((bf16[8,64,768]{2,1,0:T(8,128)(2,1)}), bf16[8,64,768]{2,1,0:T(8,128)(2,1)}, u32[]{:S(2)}, u32[]{:S(2)}) async-start(bf16[8,64,768]{2,1,0:T(8,128)(2,1)} %bitcast.614), calls=%async_computation.3 | async-start | bytes 1572864 | tf_op jit(solution)/shard_map/all_to_all | solution.py:143
  325.6 259.1 %copy-start.121 = (f32[256,8]{0,1:T(8,128)}, f32[256,8]{0,1:T(8,128)S(1)}, u32[]{:S(2)}) copy-start(f32[256,8]{0,1:T(8,128)S(1)} %get-tuple-element.60) | copy-start | bytes 24580
  346.0 12.0 %collective-permute-start.1 = (bf16[256,768]{1,0:T(8,128)(2,1)S(1)}, bf16[256,768]{1,0:T(8,128)(2,1)S(1)}, u32[]{:S(2)}, u32[]{:S(2)}) collective-permute-start(bf16[256,768]{1,0:T(8,128)(2,1)S(1)} %fusion.201), channel_id=1, source_target_pairs={{0,16},{1,17},{2,18},{3,19},{4,20},{5,21},{6,22},{7,23},{8,24},{9,... | collective-permute-start | bytes 1179656 | tf_op jit(solution)/shard_map/ppermute | solution.py:18
  383.6 22.9 %all-to-all-start.5 = ((bf16[8,64,768]{2,1,0:T(8,128)(2,1)}), bf16[8,64,768]{2,1,0:T(8,128)(2,1)}, u32[]{:S(2)}, u32[]{:S(2)}) async-start(bf16[8,64,768]{2,1,0:T(8,128)(2,1)} %bitcast.616), calls=%async_computation.5 | async-start | bytes 1572864 | tf_op jit(solution)/shard_map/all_to_all | solution.py:133
  406.5 23.9 %all-to-all-start.4 = ((bf16[8,64,768]{2,1,0:T(8,128)(2,1)}), bf16[8,64,768]{2,1,0:T(8,128)(2,1)}, u32[]{:S(2)}, u32[]{:S(2)}) async-start(bf16[8,64,768]{2,1,0:T(8,128)(2,1)} %bitcast.615), calls=%async_computation.4 | async-start | bytes 1572864 | tf_op jit(solution)/shard_map/all_to_all | solution.py:208
  430.4 24.0 %all-to-all-start.7 = ((bf16[8,64,768]{2,1,0:T(8,128)(2,1)}), bf16[8,64,768]{2,1,0:T(8,128)(2,1)}, u32[]{:S(2)}, u32[]{:S(2)}) async-start(bf16[8,64,768]{2,1,0:T(8,128)(2,1)} %bitcast.613), calls=%async_computation.7 | async-start | bytes 1572864 | tf_op jit(solution)/shard_map/all_to_all | solution.py:143
  454.4 23.9 %all-to-all-start.6 = ((bf16[8,64,768]{2,1,0:T(8,128)(2,1)}), bf16[8,64,768]{2,1,0:T(8,128)(2,1)}, u32[]{:S(2)}, u32[]{:S(2)}) async-start(bf16[8,64,768]{2,1,0:T(8,128)(2,1)} %bitcast.611), calls=%async_computation.6 | async-start | bytes 1572864 | tf_op jit(solution)/shard_map/all_to_all | solution.py:221
  499.2 12.2 %collective-permute-start.2 = (bf16[256,768]{1,0:T(8,128)(2,1)S(1)}, bf16[256,768]{1,0:T(8,128)(2,1)}, u32[]{:S(2)}, u32[]{:S(2)}) collective-permute-start(bf16[256,768]{1,0:T(8,128)(2,1)S(1)} %fusion.151), channel_id=1, source_target_pairs={{16,0},{17,1},{18,2},{19,3},{20,4},{21,5},{22,6},{23,7},{24,8},{25... | collective-permute-start | bytes 1179656 | tf_op jit(solution)/shard_map/ppermute | solution.py:18
  558.0 23.3 %all-to-all-start.9 = ((bf16[8,64,768]{2,1,0:T(8,128)(2,1)}), bf16[8,64,768]{2,1,0:T(8,128)(2,1)}, u32[]{:S(2)}, u32[]{:S(2)}) async-start(bf16[8,64,768]{2,1,0:T(8,128)(2,1)} %bitcast.617), calls=%async_computation.9 | async-start | bytes 1572864 | tf_op jit(solution)/shard_map/all_to_all | solution.py:221
  602.3 11.9 %collective-permute-start.3 = (bf16[256,768]{1,0:T(8,128)(2,1)S(1)}, bf16[256,768]{1,0:T(8,128)(2,1)S(1)}, u32[]{:S(2)}, u32[]{:S(2)}) collective-permute-start(bf16[256,768]{1,0:T(8,128)(2,1)S(1)} %get-tuple-element.40), channel_id=1, source_target_pairs={{16,0},{17,1},{18,2},{19,3},{20,4},{21,5},{22,6},{23,7},{24,8},{25... | collective-permute-start | bytes 1179656 | tf_op jit(solution)/shard_map/ppermute | solution.py:18
  653.5 22.5 %all-to-all-start.11 = ((bf16[8,64,768]{2,1,0:T(8,128)(2,1)}), bf16[8,64,768]{2,1,0:T(8,128)(2,1)S(1)}, u32[]{:S(2)}, u32[]{:S(2)}) async-start(bf16[8,64,768]{2,1,0:T(8,128)(2,1)} %bitcast.612), calls=%async_computation.11 | async-start | bytes 1572864 | tf_op jit(solution)/shard_map/all_to_all | solution.py:221
  657.0 75.2 %reduce-scatter.10.cloned.1.call-start = ((), (), s32[]{:S(2)}) async-start(), calls=%async_computation.25 | async-start | bytes 1474560 | tf_op jit(solution)/shard_map/reduce_scatter | solution.py:321
  691.8 51.6 %reduce-scatter.12.cloned.1.call-start = ((), (), s32[]{:S(2)}) async-start(), calls=%async_computation.26 | async-start | bytes 1474560 | tf_op jit(solution)/shard_map/reduce_scatter | solution.py:324
  698.3 73.4 %reduce-scatter.14.cloned.1.call-start = ((), (), s32[]{:S(2)}) async-start(), calls=%async_computation.27 | async-start | bytes 1474560 | tf_op jit(solution)/shard_map/reduce_scatter | solution.py:327
  704.5 95.5 %reduce-scatter.16.cloned.1.call-start = ((), (), s32[]{:S(2)}) async-start(), calls=%async_computation.28 | async-start | bytes 1474560 | tf_op jit(solution)/shard_map/reduce_scatter | solution.py:330
  708.1 250.2 %reduce-scatter.22.cloned.1.call-start = ((), (), s32[]{:S(2)}) async-start(), calls=%async_computation.31 | async-start | bytes 245760
  721.0 79.5 %copy-start.49 = (bf16[8,64,768]{2,1,0:T(8,128)(2,1)S(1)}, bf16[8,64,768]{2,1,0:T(8,128)(2,1)}, u32[]{:S(2)}) copy-start(bf16[8,64,768]{2,1,0:T(8,128)(2,1)} %copy-done.48) | copy-start | bytes 2359300
  721.0 330.4 %all-reduce.15.cloned.1.call-start = ((), (), s32[]{:S(2)}) async-start(), calls=%async_computation.32 | async-start | bytes 2359296 | tf_op jit(solution)/shard_map/psum | solution.py:343
  800.1 258.6 %reduce-scatter.18.cloned.1.call-start = ((), (), s32[]{:S(2)}) async-start(), calls=%async_computation.29 | async-start | bytes 11796480 | tf_op jit(solution)/shard_map/reduce_scatter | solution.py:354
  819.2 243.7 %reduce-scatter.20.cloned.1.call-start = ((), (), s32[]{:S(2)}) async-start(), calls=%async_computation.30 | async-start | bytes 11796480 | tf_op jit(solution)/shard_map/reduce_scatter | solution.py:357
  (188 other events, 1453.4 us)
Sparse Core Ops, SparseCore 0:
  9.6 20.1 all-gather.6
  31.4 17.4 all-gather.8
  50.5 17.5 all-gather.10
  69.4 17.4 all-gather.12
  88.3 64.1 all-gather.14
  154.0 64.2 all-gather.16
  691.9 22.9 reduce-scatter.9
  717.6 25.7 reduce-scatter.11
  746.0 25.7 reduce-scatter.13
  774.3 25.7 reduce-scatter.15
  803.1 19.7 reduce-scatter.21
  825.3 56.9 all-reduce.14
  884.9 78.0 reduce-scatter.17
  965.4 78.7 reduce-scatter.19
where the time goes:
time: 1090 us; the launch traced here: 1070 us
  waiting for transfers between devices  279 us (26%)
  matrix products  273 us (25%)
  local copies, waits for them, and re-layouts  237 us (22%)
  blocking collectives  136 us (12%)
  other arithmetic  83.9 us (8%)
  starting transfers between devices  45.7 us (4%)
  between operations  19 us (2%)
    unnamed x414, local copies, waits for them, and re-layouts  59.4 us
    all_gather x1, waiting for transfers between devices, local(): lax.all_gather(expert_out, 'dp', axis=2, tiled=True)  54.2 us
    rev x3, local copies, waits for them, and re-layouts, diagonal_sums(): grid_values[:, ::-1, :]  51.6 us
    all_to_all x2, blocking collectives, layer_forward(): lax.all_to_all(outgoing.reshape(experts, capacity, model_width), 'expert'...  47.5 us
    dot_general x3, matrix products, expert_backward(): jnp.einsum('necf,necd->efd', activated, grad_rows, preferred_element_type...  45.1 us
    all_to_all x2, blocking collectives, layer_backward(): lax.all_to_all(grad_outgoing.reshape(experts, capacity, model_width), 'ex...  43.9 us
    all_to_all x3, waiting for transfers between devices, layer_backward(): lax.all_to_all(grad_inputs.reshape(experts, capacity, model_width), 'expe...  42.5 us
    dot_general x3, matrix products, expert_backward(): jnp.einsum('necf,necd->efd', grad_before, inputs_all, preferred_element_t...  41.1 us
  transfers between devices with their start and end apart: 26, of which 17 were waited for; matrix products, arithmetic and copies ran while one was open for 38% of the time, Pallas kernels for 0%

commit v1 on v0

v1 whole, which is shorter than its diff:
```python
import jax
import jax.numpy as jnp
from jax import lax
from jax.experimental import pallas as pl
from jax.experimental.pallas import tpu as pltpu
from jax.sharding import PartitionSpec as P

SEQ = 256
MICRO = 2


EPSILON = 1e-06
LIMITS = (1, 2, 3, 4, 5, 6, 7, 8, 12, 16, 23, 32, 46, 64, 91)


def from_behind(block, axis, distance):
    devices = range(lax.axis_size(axis))
    route = [(i - distance, i) for i in devices if i - distance in devices]
    return lax.ppermute(block, axis, route)


def bucket_grid(length, buckets):
    positions = jnp.arange(length, dtype=jnp.int32)
    offsets = positions[:, None] - positions[None, :]
    distance = jnp.abs(offsets)
    bucket = jnp.where(offsets < 0, buckets // 2, 0).astype(jnp.int32)
    for threshold in LIMITS:
        bucket = bucket + (distance >= threshold).astype(jnp.int32)
    return bucket


def bias_of(bias_rows, length):
    buckets = bias_rows.shape[0]
    grid_values = bucket_grid(length, buckets)[None]
    bias = jnp.broadcast_to(bias_rows[0][:, None, None], (bias_rows.shape[1], length, length))
    for number in range(1, buckets):
        bias = jnp.where(grid_values == number, bias_rows[number][:, None, None], bias)
    return bias


def bucket_sums(grid_grads, buckets):
    head_count, length, _ = grid_grads.shape

    def kernel(grads_ref, table_ref):
        grid_values = bucket_grid_iota(length, buckets)
        grads = grads_ref[0]
        rows = [
            jnp.sum(jnp.where(grid_values == number, grads, 0.0), axis=0, keepdims=True)
            for number in range(buckets)
        ]
        table_ref[0] = jnp.concatenate(rows, axis=0)

    partial = pl.pallas_call(
        kernel,
        grid=(head_count,),
        out_shape=jax.ShapeDtypeStruct((head_count, buckets, length), jnp.float32),
        in_specs=[pl.BlockSpec((1, length, length), lambda h: (h, 0, 0))],
        out_specs=pl.BlockSpec((1, buckets, length), lambda h: (h, 0, 0)),
        compiler_params=pltpu.CompilerParams(vmem_limit_bytes=16 * 1024 * 1024),
        cost_estimate=pl.CostEstimate(
            flops=3 * buckets * grid_grads.size, bytes_accessed=5 * grid_grads.size, transcendentals=0
        ),
    )(grid_grads)
    return jnp.sum(partial, axis=-1).T


def bucket_grid_iota(length, buckets):
    offsets = lax.broadcasted_iota(jnp.int32, (length, length), 0) - lax.broadcasted_iota(
        jnp.int32, (length, length), 1
    )
    distance = jnp.abs(offsets)
    bucket = jnp.where(offsets < 0, buckets // 2, 0).astype(jnp.int32)
    for threshold in LIMITS:
        bucket = bucket + (distance >= threshold).astype(jnp.int32)
    return bucket


def root_scale(values):
    return lax.rsqrt(jnp.mean(values * values, axis=-1, keepdims=True) + EPSILON)


def norm_backward(grad_normed, values, factor, gain_value):
    scaled = grad_normed * gain_value
    grad_gain = jnp.sum(grad_normed * values * factor, axis=0)
    grad_values = factor * scaled - values * factor * factor * factor * jnp.mean(
        scaled * values, axis=-1, keepdims=True
    )
    return (grad_values, grad_gain)


def to_owners(outgoing, local_experts):
    experts_rows, model_width = outgoing.shape
    owners = lax.axis_size("expert")
    capacity = experts_rows // (owners * local_experts)
    received = lax.all_to_all(
        outgoing.reshape(owners, local_experts, capacity, model_width),
        "expert",
        split_axis=0,
        concat_axis=0,
        tiled=True,
    )
    return received.transpose(1, 0, 2, 3).reshape(local_experts, owners * capacity, model_width)


def to_tokens(produced):
    local_experts, rows, model_width = produced.shape
    owners = lax.axis_size("expert")
    capacity = rows // owners
    returned = lax.all_to_all(
        produced.reshape(local_experts, owners, capacity, model_width).transpose(1, 0, 2, 3),
        "expert",
        split_axis=0,
        concat_axis=0,
        tiled=True,
    )
    return returned.reshape(owners * local_experts * capacity, model_width)


def expert_forward(grouped, w_in_use, w_out_use):
    before = jnp.einsum("erd,efd->erf", grouped, w_in_use, preferred_element_type=jnp.float32)
    activated = jax.nn.gelu(before).astype(jnp.bfloat16)
    produced = jnp.einsum("erf,efd->erd", activated, w_out_use, preferred_element_type=jnp.float32)
    return (produced.astype(jnp.bfloat16), (grouped, before, activated))


def expert_backward(grad_rows, before, w_in_use, w_out_use):
    grad_activated = jnp.einsum(
        "erd,efd->erf", grad_rows, w_out_use, preferred_element_type=jnp.float32
    )
    grad_before = jax.vjp(jax.nn.gelu, before)[1](grad_activated)[0].astype(jnp.bfloat16)
    grad_inputs = jnp.einsum(
        "erf,efd->erd", grad_before, w_in_use, preferred_element_type=jnp.float32
    )
    return (grad_inputs.astype(jnp.bfloat16), grad_before)


def dispatch_of(targets, experts):
    length = targets.shape[0]
    capacity = max(2, 2 * length // experts)
    chosen = targets[:, None] == jnp.arange(experts, dtype=jnp.int32)[None, :]
    positions = jnp.arange(length, dtype=jnp.int32)
    earlier = (positions[:, None] > positions[None, :]).astype(jnp.bfloat16)
    counts = jnp.dot(earlier, chosen.astype(jnp.bfloat16), preferred_element_type=jnp.float32)
    slot_rank = jnp.sum(jnp.where(chosen, counts, 0.0), axis=-1).astype(jnp.int32)
    slot_index = targets * capacity + slot_rank
    slots = jnp.arange(experts * capacity, dtype=jnp.int32)
    placement = (slots[:, None] == slot_index[None, :]).astype(jnp.bfloat16)
    return (chosen, placement)


def place(placement, rows):
    return jnp.dot(placement, rows, preferred_element_type=jnp.float32).astype(jnp.bfloat16)


def fetch(placement, rows):
    return jnp.einsum("bs,bd->sd", placement, rows, preferred_element_type=jnp.float32)


def layer_forward(arriving, dispatch, mixer_set, position_bias, w_in_use, w_out_use):
    gain_first, gain_second, w_project, w_output, w_router = mixer_set
    hidden = arriving.astype(jnp.float32)
    length, model_width = hidden.shape
    head_count = position_bias.shape[0]
    head_size = model_width // head_count
    head_shape = (length, head_count, head_size)
    factor = head_size ** (-0.5)
    first_scale = root_scale(hidden)
    normed = (hidden * first_scale * gain_first.astype(jnp.float32)).astype(jnp.bfloat16)
    projected = jnp.dot(normed, w_project, preferred_element_type=jnp.float32).astype(jnp.bfloat16)
    queries, key_rows, value_rows = jnp.split(projected, 3, axis=1)
    scores = (
        jnp.einsum(
            "qhd,khd->hqk",
            queries.reshape(head_shape),
            key_rows.reshape(head_shape),
            preferred_element_type=jnp.float32,
        )
        * factor
        + position_bias
    )
    row_peak = jnp.max(scores, axis=-1, keepdims=True)
    log_total = row_peak + jnp.log(jnp.sum(jnp.exp(scores - row_peak), axis=-1, keepdims=True))
    shares = jnp.exp(scores - log_total).astype(jnp.bfloat16)
    attended = jnp.einsum(
        "hqk,khd->qhd", shares, value_rows.reshape(head_shape), preferred_element_type=jnp.float32
    )
    attended = attended.reshape(length, model_width).astype(jnp.bfloat16)
    mixed = hidden + jnp.dot(attended, w_output, preferred_element_type=jnp.float32)
    second_scale = root_scale(mixed)
    routed = (mixed * second_scale * gain_second.astype(jnp.float32)).astype(jnp.bfloat16)
    logits = jnp.dot(routed, w_router, preferred_element_type=jnp.float32)
    router = jax.nn.softmax(logits, axis=-1)
    chosen, placement = dispatch
    gate_value = jnp.sum(jnp.where(chosen, router, 0.0), axis=-1)
    grouped = to_owners(place(placement, routed), w_in_use.shape[0])
    produced, kept_rows = expert_forward(grouped, w_in_use, w_out_use)
    fetched = fetch(placement, to_tokens(produced))
    result = mixed + gate_value[:, None] * fetched
    stored = (
        hidden,
        normed,
        first_scale,
        queries,
        key_rows,
        value_rows,
        log_total,
        attended,
        mixed,
        second_scale,
        routed,
        router,
        chosen,
        gate_value,
        placement,
        fetched,
        kept_rows,
    )
    return (result, stored)


def layer_backward(grad_out, stored, mixer_set, position_bias, w_in_use, w_out_use):
    gain_first, gain_second, w_project, w_output, w_router = mixer_set
    (
        hidden,
        normed,
        first_scale,
        queries,
        key_rows,
        value_rows,
        log_total,
        attended,
        mixed,
        second_scale,
        routed,
        router,
        chosen,
        gate_value,
        placement,
        fetched,
        kept_rows,
    ) = stored
    length, model_width = hidden.shape
    head_count = position_bias.shape[0]
    head_size = model_width // head_count
    head_shape = (length, head_count, head_size)
    factor = head_size ** (-0.5)
    grad_gate = jnp.sum(grad_out * fetched, axis=-1)
    grad_fetched = (gate_value[:, None] * grad_out).astype(jnp.bfloat16)
    grouped, before, activated = kept_rows
    grad_rows = to_owners(place(placement, grad_fetched), w_in_use.shape[0])
    grad_inputs, grad_before = expert_backward(grad_rows, before, w_in_use, w_out_use)
    grad_routed = fetch(placement, to_tokens(grad_inputs))
    grad_logits = (
        (gate_value * grad_gate)[:, None] * (chosen.astype(jnp.float32) - router)
    ).astype(jnp.bfloat16)
    grad_routed = grad_routed + jnp.einsum(
        "se,de->sd", grad_logits, w_router, preferred_element_type=jnp.float32
    )
    norm_grad, grad_gain_second = norm_backward(
        grad_routed, mixed, second_scale, gain_second.astype(jnp.float32)
    )
    grad_mixed = grad_out + norm_grad
    grad_branch = grad_mixed.astype(jnp.bfloat16)
    grad_attended = jnp.einsum(
        "se,de->sd", grad_branch, w_output, preferred_element_type=jnp.float32
    )
    grad_attended = grad_attended.astype(jnp.bfloat16).reshape(head_shape)
    query_heads = queries.reshape(head_shape)
    key_heads = key_rows.reshape(head_shape)
    scores = (
        jnp.einsum("qhd,khd->hqk", query_heads, key_heads, preferred_element_type=jnp.float32)
        * factor
        + position_bias
    )
    softmax_rows = jnp.exp(scores - log_total)
    shares = softmax_rows.astype(jnp.bfloat16)
    grad_values = jnp.einsum(
        "hqk,qhd->khd", shares, grad_attended, preferred_element_type=jnp.float32
    )
    grad_values = grad_values.astype(jnp.bfloat16).reshape(length, model_width)
    grad_shares = jnp.einsum(
        "qhd,khd->hqk",
        grad_attended,
        value_rows.reshape(head_shape),
        preferred_element_type=jnp.float32,
    )
    grad_scores = softmax_rows * (
        grad_shares - jnp.sum(grad_shares * softmax_rows, axis=-1, keepdims=True)
    )
    grad_scores = grad_scores.astype(jnp.bfloat16)
    grad_queries = (
        jnp.einsum("hqk,khd->qhd", grad_scores, key_heads, preferred_element_type=jnp.float32)
        * factor
    )
    grad_queries = grad_queries.astype(jnp.bfloat16).reshape(length, model_width)
    grad_keys = (
        jnp.einsum("hqk,qhd->khd", grad_scores, query_heads, preferred_element_type=jnp.float32)
        * factor
    )
    grad_keys = grad_keys.astype(jnp.bfloat16).reshape(length, model_width)
    grad_projected = jnp.concatenate([grad_queries, grad_keys, grad_values], axis=1)
    grad_normed = jnp.einsum(
        "se,de->sd", grad_projected, w_project, preferred_element_type=jnp.float32
    )
    first_grad, grad_gain_first = norm_backward(
        grad_normed, hidden, first_scale, gain_first.astype(jnp.float32)
    )
    grad_hidden = grad_mixed + first_grad
    kept = dict(
        gains=jnp.stack([grad_gain_first, grad_gain_second], axis=1),
        grad_scores=grad_scores,
        normed=normed,
        grad_projected=grad_projected,
        attended=attended,
        grad_branch=grad_branch,
        routed=routed,
        grad_logits=grad_logits,
    )
    return (grad_hidden, kept, dict(
        grouped=grouped, activated=activated, grad_rows=grad_rows, grad_before=grad_before
    ))


def scatter_sum(full, axis):
    return lax.psum_scatter(full, "dp", scatter_dimension=axis, tiled=True)


def weight_grad(operands, grads):
    return jnp.einsum("sd,se->de", operands, grads, preferred_element_type=jnp.float32)


def reduce_mixer(rows, sums, buckets):
    project = weight_grad(rows["normed"], rows["grad_projected"])
    output = weight_grad(rows["attended"], rows["grad_branch"])
    router = weight_grad(rows["routed"], rows["grad_logits"])
    table = bucket_sums(sums["grad_scores"], buckets)
    small = pack_small([router, sums["gains"]], table)
    packed = jnp.concatenate([project, output, small], axis=1).astype(jnp.bfloat16)
    total = lax.psum(scatter_sum(packed, 0), "expert").astype(jnp.float32)
    width = total.shape[0] * lax.axis_size("dp")
    query, key, value, output = (total[:, i * width : (i + 1) * width] for i in range(4))
    router, gains, table = unpack_small(
        total[:, 4 * width :], [router.shape[1], 2], table.shape, 1
    )
    return (gains[:, 0], gains[:, 1], query, key, value, output, router, table)


def pack_small(columns, table, shards=None):
    rows = columns[0].shape[0]
    shards = lax.axis_size("dp") if shards is None else shards
    own = table.reshape(shards, table.shape[0] // shards, table.shape[1])
    own = jnp.pad(own, ((0, 0), (0, rows // shards - own.shape[1]), (0, 0)))
    packed = jnp.concatenate([*columns, own.reshape(rows, table.shape[1])], axis=1)
    return jnp.pad(packed, ((0, 0), (0, -packed.shape[1] % 128)))


def unpack_small(packed, widths, table_shape, shards):
    found = []
    start = 0
    for width in widths:
        found.append(packed[:, start : start + width])
        start += width
    table_rows, heads = table_shape
    table_rows = table_rows * shards // lax.axis_size("dp")
    table = packed[:, start : start + heads].reshape(shards, -1, heads)
    found.append(table[:, : table_rows // shards].reshape(table_rows, heads))
    return found


def local(
    ends,
    routes,
    norm_gain_first,
    norm_gain_second,
    w_query,
    w_key,
    w_value,
    w_output,
    w_router,
    bias_table,
    expert_in,
    expert_out,
):
    is_first = lax.axis_index("section") == 0
    model_width = ends.shape[2]
    shards = lax.axis_size("dp")
    experts = w_router.shape[2]
    gains = jnp.stack([norm_gain_first[0], norm_gain_second[0]], axis=1)
    small = pack_small([w_router[0], gains], bias_table[0], 1)
    packed = jnp.concatenate([w_query[0], w_key[0], w_value[0], w_output[0], small], axis=1)
    packed = lax.all_gather(packed, "dp", axis=0, tiled=True)
    w_in_use = lax.all_gather(expert_in[0], "dp", axis=1, tiled=True)
    w_out_use = lax.all_gather(expert_out[0], "dp", axis=1, tiled=True)
    buckets = bias_table.shape[1] * shards
    router_full, gains, bias_rows = unpack_small(
        packed[:, 4 * model_width :],
        [experts, 2],
        (buckets * shards // shards, bias_table.shape[2]),
        shards,
    )
    mixer_set = (
        gains[:, 0],
        gains[:, 1],
        packed[:, : 3 * model_width],
        packed[:, 3 * model_width : 4 * model_width],
        router_full,
    )
    position_bias = bias_of(bias_rows.astype(jnp.float32), SEQ)
    local_rows = ends[0]
    local_routes = routes[0, :, 0]

    def block_rows(source, micro_index):
        return source[micro_index * SEQ : (micro_index + 1) * SEQ]

    dispatches = [dispatch_of(block_rows(local_routes, m), experts) for m in range(MICRO)]
    stored_list = []
    results = []
    arriving = jnp.zeros((SEQ, model_width), jnp.bfloat16)
    for tick_number in range(MICRO + 1):
        own_micro = min(tick_number, MICRO - 1)
        prior_micro = max(tick_number - 1, 0)
        layer_input = jnp.where(is_first, block_rows(local_rows, own_micro), arriving)
        dispatch = jax.tree.map(
            lambda own, prior: jnp.where(is_first, own, prior),
            dispatches[own_micro],
            dispatches[prior_micro],
        )
        result, stored = layer_forward(
            layer_input, dispatch, mixer_set, position_bias, w_in_use, w_out_use
        )
        stored_list.append(stored)
        results.append(result)
        if tick_number < MICRO:
            arriving = from_behind(result.astype(jnp.bfloat16), "section", 1)
    input_grads = [None] * MICRO
    returning = jnp.zeros((SEQ, model_width), jnp.bfloat16)
    mixer_kept = []
    expert_kept = []
    for step_number in range(MICRO + 1):
        if step_number < MICRO:
            cotangent = block_rows(local_rows, MICRO - 1 - step_number).astype(jnp.float32)
        else:
            cotangent = jnp.zeros((SEQ, model_width), jnp.float32)
        grad_out = jnp.where(is_first, returning.astype(jnp.float32), cotangent)
        grad_hidden, kept_mixer, kept_expert = layer_backward(
            grad_out,
            stored_list[MICRO - step_number],
            mixer_set,
            position_bias,
            w_in_use,
            w_out_use,
        )
        if step_number < MICRO:
            returning = from_behind(grad_hidden.astype(jnp.bfloat16), "section", -1)
        if step_number >= 1:
            input_grads[MICRO - step_number] = grad_hidden
        mixer_kept.append(kept_mixer)
        expert_kept.append(kept_expert)

    def real(kept, name):
        return (kept[1][name], jnp.where(is_first, kept[2][name], kept[0][name]))

    experts_rows = {
        name: jnp.concatenate(real(expert_kept, name), axis=1) for name in expert_kept[0]
    }
    grad_out_full = jnp.einsum(
        "erf,erd->efd",
        experts_rows["activated"],
        experts_rows["grad_rows"],
        preferred_element_type=jnp.float32,
    )
    grad_w_out = scatter_sum(grad_out_full.astype(jnp.bfloat16), 1).astype(jnp.float32)
    grad_in_full = jnp.einsum(
        "erf,erd->efd",
        experts_rows["grad_before"],
        experts_rows["grouped"],
        preferred_element_type=jnp.float32,
    )
    grad_w_in = scatter_sum(grad_in_full.astype(jnp.bfloat16), 1).astype(jnp.float32)
    expert_sum = (grad_w_in, grad_w_out)
    summed = ("gains", "grad_scores")
    sums = {
        name: sum(part.astype(jnp.float32) for part in real(mixer_kept, name)) for name in summed
    }
    rows = {
        name: jnp.concatenate(real(mixer_kept, name), axis=0)
        for name in mixer_kept[0]
        if name not in summed
    }
    mixer_sum = reduce_mixer(rows, sums, buckets)
    pieces = [
        jnp.where(is_first, input_grads[micro_index], results[micro_index + 1])
        for micro_index in range(MICRO)
    ]
    boundary = jnp.concatenate(pieces, axis=0)[None]
    return (
        boundary,
        mixer_sum[0][None],
        mixer_sum[1][None],
        mixer_sum[2][None],
        mixer_sum[3][None],
        mixer_sum[4][None],
        mixer_sum[5][None],
        mixer_sum[6][None],
        mixer_sum[7][None],
        expert_sum[0][None],
        expert_sum[1][None],
    )


def solution(mesh):
    in_specs = (
        P("section", ("expert", "dp"), None),
        P("section", ("expert", "dp"), None),
        P("section", "dp"),
        P("section", "dp"),
        P("section", "dp", None),
        P("section", "dp", None),
        P("section", "dp", None),
        P("section", "dp", None),
        P("section", "dp", None),
        P("section", "dp", None),
        P("section", "expert", "dp", None),
        P("section", "expert", "dp", None),
    )
    out_specs = (
        P("section", ("expert", "dp"), None),
        P("section", "dp"),
        P("section", "dp"),
        P("section", "dp", None),
        P("section", "dp", None),
        P("section", "dp", None),
        P("section", "dp", None),
        P("section", "dp", None),
        P("section", "dp", None),
        P("section", "expert", "dp", None),
        P("section", "expert", "dp", None),
    )
    return jax.shard_map(local, mesh=mesh, in_specs=in_specs, out_specs=out_specs, check_vma=False)
```

time: 1090 us -> 980 us (0.90)
  waiting for transfers between devices: 279 us -> 460 us
  local copies, waits for them, and re-layouts: 237 us -> 63.1 us
  matrix products: 273 us -> 203 us
  blocking collectives: 136 us -> 88.8 us
  Pallas kernels: 0 us -> 13.3 us
    reduce_scatter x6 -> x3, waiting for transfers between devices: 67.9 us -> 199 us  [scatter_sum(): return lax.psum_scatter(full, 'dp', scatter_dimension=axis, tiled=True)]
    dot_general x53 -> x37, matrix products: 236 us -> 155 us  [the longest x3 28 us: expert_backward(): jnp.einsum('erd,efd->erf', grad_rows, w_out_use, preferred_element_type=j...]
    rev x4 -> x0, local copies, waits for them, and re-layouts: 74 us -> none  [the longest x3 51.6 us: diagonal_sums(): grid_values[:, ::-1, :]]
    unnamed x414 -> x355, local copies, waits for them, and re-layouts: 59.4 us -> 22.5 us
    psum x1, waiting for transfers between devices: 0.01 us -> 34.6 us  [reduce_mixer(): total = lax.psum(scatter_sum(packed, 0), 'expert').astype(jnp.float32)]
    reshape x4 -> x8, local copies, waits for them, and re-layouts: 37.1 us -> 5.69 us  [the longest x6 5.6 us: to_tokens(): produced.reshape(local_experts, owners, capacity, model_width)]
    unnamed x2 -> x0, blocking collectives: 20.6 us -> none
    select_n x3 -> x9, other arithmetic: 0.61 us -> 20.2 us  [the longest x1 12.7 us: bias_of(): jnp.where(grid_values == number, bias_rows[number][:, None, None], bias)]
  transfers between devices with their start and end apart: 26 -> 19, of which waited for: 17 -> 19; matrix products, arithmetic and copies ran while one was open for 38% -> 14% of each run, Pallas kernels for 0% -> 0%
where the time goes in v1:
time: 980 us; the launch traced here: 968 us
  waiting for transfers between devices  460 us (47%)
  matrix products  203 us (21%)
  blocking collectives  88.8 us (9%)
  other arithmetic  77.1 us (8%)
  local copies, waits for them, and re-layouts  63.1 us (6%)
  starting transfers between devices  45.9 us (5%)
  between operations  16.8 us (2%)
  Pallas kernels  13.3 us (1%)
    reduce_scatter x3, waiting for transfers between devices, scatter_sum(): return lax.psum_scatter(full, 'dp', scatter_dimension=axis, tiled=True)  199 us
    all_to_all x4, blocking collectives, to_owners(): lax.all_to_all(outgoing.reshape(owners, local_experts, capacity, model_wi...  88.8 us
    all_to_all x6, waiting for transfers between devices, to_tokens(): lax.all_to_all(produced.reshape(local_experts, owners, capacity, model_wi...  67.8 us
    all_gather x1, waiting for transfers between devices, local(): w_out_use = lax.all_gather(expert_out[0], 'dp', axis=1, tiled=True)  54.2 us
    ppermute x4, waiting for transfers between devices, from_behind(): return lax.ppermute(block, axis, route)  35.5 us
    psum x1, waiting for transfers between devices, reduce_mixer(): total = lax.psum(scatter_sum(packed, 0), 'expert').astype(jnp.float32)  34.6 us
    all_to_all x2, waiting for transfers between devices, to_owners(): lax.all_to_all(outgoing.reshape(owners, local_experts, capacity, model_wi...  30.2 us
    dot_general x3, matrix products, expert_backward(): jnp.einsum('erd,efd->erf', grad_rows, w_out_use, preferred_element_type=j...  28 us
  transfers between devices with their start and end apart: 19, of which 19 were waited for; matrix products, arithmetic and copies ran while one was open for 14% of the time, Pallas kernels for 0%

profile of v1, /device:TPU:0, one launch (start us, length us, event | category | flops | bytes accessed | tf_op | source)
XLA Modules:
  0.0 968.1 jit_solution(906908953142831470)
XLA Ops:
  33.9 21.4 %all-gather.6.cloned.1.call-done = bf16[768,3200]{1,0:T(8,128)(2,1)} async-done(((bf16[192,3200]{1,0:T(8,128)(2,1)}), bf16[768,3200]{1,0:T(8,128)(2,1)}) %all-gather.6.cloned.1.call-update) | async-done | bytes 4915216 | tf_op jit(solution)/shard_map/all_gather | solution.py:391
  62.0 12.7 %select_select_fusion = f32[12,256,256]{2,1,0:T(8,128)S(1)} fusion(f32[12]{0:T(128)S(1)} %get-tuple-element.123, f32[12]{0:T(128)S(1)} %get-tuple-element.124, f32[12]{0:T(128)S(1)} %get-tuple-element.125, f32[12]{0:T(128)S(1)} %get-tuple-element.126, f32[12]{0:T(128)S(1)} %get-tuple-element.127, f32[12]{0:T(128)S(1)} %get-tuple-element.128, ...), kind=kLoop, calls=%fused_computation.82 | loop fusion | flops 24379392 | bytes 5178880 | tf_op jit(solution)/shard_map/jit(_where)/select_n | solution.py:37
  80.6 24.9 %all_to_all.60 = bf16[4,2,64,768]{3,2,1,0:T(8,128)(2,1)S(1)} all-to-all(bf16[4,2,64,768]{3,2,1,0:T(8,128)(2,1)S(1)} %bitcast.405), channel_id=1, replica_groups=mesh['section'=2,'expert'=4,'dp'=4] {'expert'}, dimensions={0} | all-to-all | bytes 1572864 | tf_op jit(solution)/shard_map/all_to_all | solution.py:95
  105.7 15.5 %all-gather.8.cloned.1.call-done = bf16[1,2,3072,768]{3,2,1,0:T(8,128)(2,1)} async-done(((bf16[1,2,768,768]{3,2,1,0:T(8,128)(2,1)}), bf16[1,2,3072,768]{3,2,1,0:T(8,128)(2,1)}) %all-gather.8.cloned.1.call-update) | async-done | bytes 9437200 | tf_op jit(solution)/shard_map/all_gather | solution.py:392
  121.2 11.6 %fusion.22 = f32[2,256,3072]{2,1,0:T(8,128)} fusion(bf16[2,256,768]{2,1,0:T(8,128)(2,1)S(1)} %bitcast.358, bf16[1,2,3072,768]{3,2,1,0:T(8,128)(2,1)} %all-gather.8.cloned.1.call-done), kind=kOutput, calls=%fused_computation.22 | convolution fusion | flops 2415919104 | bytes 16515072 | tf_op jit(solution)/shard_map/erd,efd->erf/dot_general | solution.py:120
  132.8 54.2 %all-gather.10.cloned.1.call-done = bf16[1,2,3072,768]{3,2,1,0:T(8,128)(2,1)} async-done(((bf16[1,2,768,768]{3,2,1,0:T(8,128)(2,1)}), bf16[1,2,3072,768]{3,2,1,0:T(8,128)(2,1)}) %all-gather.10.cloned.1.call-update) | async-done | bytes 9437200 | tf_op jit(solution)/shard_map/all_gather | solution.py:393
  187.0 8.5 fusion.91
  202.3 19.2 %all-to-all-done.1 = bf16[4,2,64,768]{3,2,1,0:T(8,128)(2,1)S(1)} async-done(((bf16[4,2,64,768]{3,2,1,0:T(8,128)(2,1)}), bf16[4,2,64,768]{3,2,1,0:T(8,128)(2,1)S(1)}, u32[]{:S(2)}, u32[]{:S(2)}) %all-to-all-start.1) | async-done | bytes 786464 | tf_op jit(solution)/shard_map/all_to_all | solution.py:109
  249.1 21.2 %all_to_all.61 = bf16[4,2,64,768]{3,2,1,0:T(8,128)(2,1)S(1)} all-to-all(bf16[4,2,64,768]{3,2,1,0:T(8,128)(2,1)S(1)} %bitcast.431), channel_id=1, replica_groups=mesh['section'=2,'expert'=4,'dp'=4] {'expert'}, dimensions={0} | all-to-all | bytes 1572864 | tf_op jit(solution)/shard_map/all_to_all | solution.py:95
  275.5 7.5 fusion.94
  291.9 15.3 %all-to-all-done.3 = bf16[4,2,64,768]{3,2,1,0:T(8,128)(2,1)} async-done(((bf16[4,2,64,768]{3,2,1,0:T(8,128)(2,1)}), bf16[4,2,64,768]{3,2,1,0:T(8,128)(2,1)}, u32[]{:S(2)}, u32[]{:S(2)}) %all-to-all-start.3) | async-done | bytes 786464 | tf_op jit(solution)/shard_map/all_to_all | solution.py:109
  357.4 12.6 %all-to-all-done.5 = bf16[4,2,64,768]{3,2,1,0:T(8,128)(2,1)} async-done(((bf16[4,2,64,768]{3,2,1,0:T(8,128)(2,1)}), bf16[4,2,64,768]{3,2,1,0:T(8,128)(2,1)}, u32[]{:S(2)}, u32[]{:S(2)}) %all-to-all-start.5) | async-done | bytes 786464 | tf_op jit(solution)/shard_map/all_to_all | solution.py:95
  376.4 17.6 %all-to-all-done.4 = bf16[4,2,64,768]{3,2,1,0:T(8,128)(2,1)} async-done(((bf16[4,2,64,768]{3,2,1,0:T(8,128)(2,1)}), bf16[4,2,64,768]{3,2,1,0:T(8,128)(2,1)}, u32[]{:S(2)}, u32[]{:S(2)}) %all-to-all-start.4) | async-done | bytes 786464 | tf_op jit(solution)/shard_map/all_to_all | solution.py:95
  396.0 9.8 %broadcast_select_fusion = (bf16[2,256,3072]{2,1,0:T(8,128)(2,1)}, f32[2,256,3072]{2,1,0:T(8,128)S(1)}) fusion(pred[]{:T(512)S(6)} %eq.378, f32[2,256,3072]{2,1,0:T(8,128)} %fusion.22, bf16[2,256,768]{2,1,0:T(8,128)(2,1)} %bitcast.391, bf16[1,2,3072,768]{3,2,1,0:T(8,128)(2,1)} %all-gather.8.cloned.1.call-done), kind=kOutput, calls=%fused_computation.84 | convolution fusion | flops 2445803520 | bytes 25952256 | tf_op jit(solution)/shard_map/erd,efd->erf/dot_general | solution.py:120
  405.8 9.1 fusion.97
  420.5 8.9 fusion.44
  429.4 7.5 fusion.82
  450.4 13.7 %all-to-all-done.6 = bf16[4,2,64,768]{3,2,1,0:T(8,128)(2,1)} async-done(((bf16[4,2,64,768]{3,2,1,0:T(8,128)(2,1)}), bf16[4,2,64,768]{3,2,1,0:T(8,128)(2,1)}, u32[]{:S(2)}, u32[]{:S(2)}) %all-to-all-start.6) | async-done | bytes 786464 | tf_op jit(solution)/shard_map/all_to_all | solution.py:109
  484.1 10.8 %collective-permute-done.2 = bf16[256,768]{1,0:T(8,128)(2,1)S(1)} collective-permute-done((bf16[256,768]{1,0:T(8,128)(2,1)S(1)}, bf16[256,768]{1,0:T(8,128)(2,1)S(1)}, u32[]{:S(2)}, u32[]{:S(2)}) %collective-permute-start.2) | collective-permute-done | bytes 393248 | tf_op jit(solution)/shard_map/ppermute | solution.py:19
  495.4 21.7 %all_to_all.62 = bf16[4,2,64,768]{3,2,1,0:T(8,128)(2,1)S(1)} all-to-all(bf16[4,2,64,768]{3,2,1,0:T(8,128)(2,1)S(1)} %bitcast.435), channel_id=1, replica_groups=mesh['section'=2,'expert'=4,'dp'=4] {'expert'}, dimensions={0} | all-to-all | bytes 1572864 | tf_op jit(solution)/shard_map/all_to_all | solution.py:95
  517.2 8.8 fusion.37
  539.3 15.5 %all-to-all-done.9 = bf16[4,2,64,768]{3,2,1,0:T(8,128)(2,1)} async-done(((bf16[4,2,64,768]{3,2,1,0:T(8,128)(2,1)}), bf16[4,2,64,768]{3,2,1,0:T(8,128)(2,1)}, u32[]{:S(2)}, u32[]{:S(2)}) %all-to-all-start.9) | async-done | bytes 786464 | tf_op jit(solution)/shard_map/all_to_all | solution.py:109
  576.3 10.7 %collective-permute-done.3 = bf16[256,768]{1,0:T(8,128)(2,1)S(1)} collective-permute-done((bf16[256,768]{1,0:T(8,128)(2,1)S(1)}, bf16[256,768]{1,0:T(8,128)(2,1)S(1)}, u32[]{:S(2)}, u32[]{:S(2)}) %collective-permute-start.3) | collective-permute-done | bytes 393248 | tf_op jit(solution)/shard_map/ppermute | solution.py:19
  587.8 21.1 %all_to_all.63 = bf16[4,2,64,768]{3,2,1,0:T(8,128)(2,1)S(1)} all-to-all(bf16[4,2,64,768]{3,2,1,0:T(8,128)(2,1)S(1)} %bitcast.437), channel_id=1, replica_groups=mesh['section'=2,'expert'=4,'dp'=4] {'expert'}, dimensions={0} | all-to-all | bytes 1572864 | tf_op jit(solution)/shard_map/all_to_all | solution.py:95
  609.0 10.3 %broadcast_select_fusion.1 = (bf16[2,256,3072]{2,1,0:T(8,128)(2,1)}, bf16[2,256,3072]{2,1,0:T(8,128)(2,1)}) fusion(bf16[2,256,3072]{2,1,0:T(8,128)(2,1)} %copy-done.152, pred[]{:T(512)S(6)} %eq.378, f32[2,256,3072]{2,1,0:T(8,128)S(1)} %bitcast.360, bf16[2,256,768]{2,1,0:T(8,128)(2,1)S(1)} %bitcast.393, ...), kind=kOutput, calls=%fused_computation.85 | convolution fusion | flops 2448949248 | bytes 25952256 | tf_op jit(solution)/shard_map/erd,efd->erf/dot_general | solution.py:127
  662.8 13.3 %shard_map.203 = f32[12,32,256]{2,1,0:T(8,128)S(1)} custom-call(f32[12,256,256]{2,1,0:T(8,128)S(1)} %get-tuple-element.99.grads_ref), custom_call_target="tpu_custom_call" | custom-call | flops 75497472 | bytes 3932160 | tf_op jit(solution)/shard_map/pallas_call | solution.py:53
  688.0 47.2 %reduce-scatter.4.cloned.1.call-done = bf16[192,3200]{1,0:T(8,128)(2,1)} async-done(((bf16[768,3200]{1,0:T(8,128)(2,1)}), bf16[192,3200]{1,0:T(8,128)(2,1)}) %reduce-scatter.4.cloned.1.call-update) | async-done | bytes 1228816 | tf_op jit(solution)/shard_map/reduce_scatter | solution.py:325
  735.8 9.5 convolution_convert_fusion
  746.9 9.3 convolution_convert_fusion.1
  760.7 34.6 %all-reduce.6.cloned.1.call-done = bf16[192,3200]{1,0:T(8,128)(2,1)} async-done(((bf16[192,3200]{1,0:T(8,128)(2,1)}), bf16[192,3200]{1,0:T(8,128)(2,1)}) %all-reduce.6.cloned.1.call-update) | async-done | bytes 1228816 | tf_op jit(solution)/shard_map/psum | solution.py:339
  800.4 75.5 %reduce-scatter.8.cloned.1.call-done = bf16[2,768,768]{2,1,0:T(8,128)(2,1)} async-done(((bf16[2,3072,768]{2,1,0:T(8,128)(2,1)}), bf16[2,768,768]{2,1,0:T(8,128)(2,1)}) %reduce-scatter.8.cloned.1.call-update) | async-done | bytes 2359312 | tf_op jit(solution)/shard_map/reduce_scatter | solution.py:325
  880.1 76.8 %reduce-scatter.6.cloned.1.call-done = bf16[2,768,768]{2,1,0:T(8,128)(2,1)} async-done(((bf16[2,3072,768]{2,1,0:T(8,128)(2,1)}), bf16[2,768,768]{2,1,0:T(8,128)(2,1)}) %reduce-scatter.6.cloned.1.call-update) | async-done | bytes 2359312 | tf_op jit(solution)/shard_map/reduce_scatter | solution.py:325
  (601 shorter events, 295.0 us)
Async XLA Ops:
  7.2 48.2 %all-gather.6.cloned.1.call-start = ((), (), s32[]{:S(2)}) async-start(), calls=%async_computation.15 | async-start | bytes 6144000 | tf_op jit(solution)/shard_map/all_gather | solution.py:391
  13.9 107.2 %all-gather.8.cloned.1.call-start = ((), (), s32[]{:S(2)}) async-start(), calls=%async_computation.20 | async-start | bytes 11796480 | tf_op jit(solution)/shard_map/all_gather | solution.py:392
  14.7 172.3 %all-gather.10.cloned.1.call-start = ((), (), s32[]{:S(2)}) async-start(), calls=%async_computation.21 | async-start | bytes 11796480 | tf_op jit(solution)/shard_map/all_gather | solution.py:393
  32.9 169.3 %copy-start.111 = (s32[1,256,1]{1,2,0:T(1,128)}, s32[1,256,1]{1,2,0:T(1,128)S(1)}, u32[]{:S(2)}) copy-start(s32[1,256,1]{1,2,0:T(1,128)S(1)} %get-tuple-element.155) | copy-start | bytes 3076
  32.9 193.7 %copy-start.110 = (s32[1,256,1]{1,2,0:T(1,128)}, s32[1,256,1]{1,2,0:T(1,128)S(1)}, u32[]{:S(2)}) copy-start(s32[1,256,1]{1,2,0:T(1,128)S(1)} %get-tuple-element.154) | copy-start | bytes 3076
  56.7 177.5 %copy-start.103 = (f32[768]{0:T(1024)}, f32[768]{0:T(1024)S(1)}, u32[]{:S(2)}) copy-start(f32[768]{0:T(1024)S(1)} %get-tuple-element.78) | copy-start | bytes 9220
  80.1 141.5 %copy-start.9 = (f32[256,768]{1,0:T(8,128)}, f32[256,768]{1,0:T(8,128)S(1)}, u32[]{:S(2)}) copy-start(f32[256,768]{1,0:T(8,128)S(1)} %get-tuple-element.159) | copy-start | bytes 2359300
  80.1 52.7 %copy-start.117 = (f32[256]{0:T(256)}, f32[256]{0:T(256)S(1)}, u32[]{:S(2)}) copy-start(f32[256]{0:T(256)S(1)} %add_rsqrt_fusion.4) | copy-start | bytes 3076
  196.4 25.1 %all-to-all-start.1 = ((bf16[4,2,64,768]{3,2,1,0:T(8,128)(2,1)}), bf16[4,2,64,768]{3,2,1,0:T(8,128)(2,1)S(1)}, u32[]{:S(2)}, u32[]{:S(2)}) async-start(bf16[4,2,64,768]{3,2,1,0:T(8,128)(2,1)} %bitcast.351), calls=%async_computation.1 | async-start | bytes 1572864 | tf_op jit(solution)/shard_map/all_to_all | solution.py:109
  222.9 11.0 %collective-permute-start = (bf16[256,768]{1,0:T(8,128)(2,1)S(1)}, bf16[256,768]{1,0:T(8,128)(2,1)S(1)}, u32[]{:S(2)}, u32[]{:S(2)}) collective-permute-start(bf16[256,768]{1,0:T(8,128)(2,1)S(1)} %get-tuple-element.162), channel_id=1, source_target_pairs={{0,16},{1,17},{2,18},{3,19},{4,20},{5,21},{6,22},{7,23},{8,24},{9,... | collective-permute-start | bytes 1179656 | tf_op jit(solution)/shard_map/ppermute | solution.py:19
  283.9 23.3 %all-to-all-start.3 = ((bf16[4,2,64,768]{3,2,1,0:T(8,128)(2,1)}), bf16[4,2,64,768]{3,2,1,0:T(8,128)(2,1)}, u32[]{:S(2)}, u32[]{:S(2)}) async-start(bf16[4,2,64,768]{3,2,1,0:T(8,128)(2,1)} %bitcast.396), calls=%async_computation.3 | async-start | bytes 1572864 | tf_op jit(solution)/shard_map/all_to_all | solution.py:109
  309.9 11.9 %collective-permute-start.1 = (bf16[256,768]{1,0:T(8,128)(2,1)S(1)}, bf16[256,768]{1,0:T(8,128)(2,1)S(1)}, u32[]{:S(2)}, u32[]{:S(2)}) collective-permute-start(bf16[256,768]{1,0:T(8,128)(2,1)S(1)} %get-tuple-element.172), channel_id=1, source_target_pairs={{0,16},{1,17},{2,18},{3,19},{4,20},{5,21},{6,22},{7,23},{8,24},{9,... | collective-permute-start | bytes 1179656 | tf_op jit(solution)/shard_map/ppermute | solution.py:19
  347.1 22.9 %all-to-all-start.5 = ((bf16[4,2,64,768]{3,2,1,0:T(8,128)(2,1)}), bf16[4,2,64,768]{3,2,1,0:T(8,128)(2,1)}, u32[]{:S(2)}, u32[]{:S(2)}) async-start(bf16[4,2,64,768]{3,2,1,0:T(8,128)(2,1)} %bitcast.404), calls=%async_computation.5 | async-start | bytes 1572864 | tf_op jit(solution)/shard_map/all_to_all | solution.py:95
  370.1 23.9 %all-to-all-start.4 = ((bf16[4,2,64,768]{3,2,1,0:T(8,128)(2,1)}), bf16[4,2,64,768]{3,2,1,0:T(8,128)(2,1)}, u32[]{:S(2)}, u32[]{:S(2)}) async-start(bf16[4,2,64,768]{3,2,1,0:T(8,128)(2,1)} %bitcast.428), calls=%async_computation.4 | async-start | bytes 1572864 | tf_op jit(solution)/shard_map/all_to_all | solution.py:95
  415.9 24.3 %all-to-all-start.7 = ((bf16[4,2,64,768]{3,2,1,0:T(8,128)(2,1)}), bf16[4,2,64,768]{3,2,1,0:T(8,128)(2,1)}, u32[]{:S(2)}, u32[]{:S(2)}) async-start(bf16[4,2,64,768]{3,2,1,0:T(8,128)(2,1)} %bitcast.397), calls=%async_computation.7 | async-start | bytes 1572864 | tf_op jit(solution)/shard_map/all_to_all | solution.py:109
  440.2 23.9 %all-to-all-start.6 = ((bf16[4,2,64,768]{3,2,1,0:T(8,128)(2,1)}), bf16[4,2,64,768]{3,2,1,0:T(8,128)(2,1)}, u32[]{:S(2)}, u32[]{:S(2)}) async-start(bf16[4,2,64,768]{3,2,1,0:T(8,128)(2,1)} %bitcast.394), calls=%async_computation.6 | async-start | bytes 1572864 | tf_op jit(solution)/shard_map/all_to_all | solution.py:109
  480.3 36.9 %slice-start.17 = ((s8[9437184]{0:T(1024)(128)(4,1)}), s8[4194304]{0:T(1024)(128)(4,1)S(1)}, s32[]{:S(2)}) async-start(s8[9437184]{0:T(1024)(128)(4,1)} %bitcast.466), calls=%async_computation.39 | async-start | bytes 8388608
  480.3 36.9 %slice-start.18 = ((s8[9437184]{0:T(1024)(128)(4,1)}), s8[4194304]{0:T(1024)(128)(4,1)S(1)}, s32[]{:S(2)}) async-start(s8[9437184]{0:T(1024)(128)(4,1)} %bitcast.466), calls=%async_computation.40 | async-start | bytes 8388608
  482.5 12.4 %collective-permute-start.2 = (bf16[256,768]{1,0:T(8,128)(2,1)S(1)}, bf16[256,768]{1,0:T(8,128)(2,1)S(1)}, u32[]{:S(2)}, u32[]{:S(2)}) collective-permute-start(bf16[256,768]{1,0:T(8,128)(2,1)S(1)} %fusion.130), channel_id=1, source_target_pairs={{16,0},{17,1},{18,2},{19,3},{20,4},{21,5},{22,6},{23,7},{24,8},{25... | collective-permute-start | bytes 1179656 | tf_op jit(solution)/shard_map/ppermute | solution.py:19
  531.6 23.3 %all-to-all-start.9 = ((bf16[4,2,64,768]{3,2,1,0:T(8,128)(2,1)}), bf16[4,2,64,768]{3,2,1,0:T(8,128)(2,1)}, u32[]{:S(2)}, u32[]{:S(2)}) async-start(bf16[4,2,64,768]{3,2,1,0:T(8,128)(2,1)} %bitcast.395), calls=%async_computation.9 | async-start | bytes 1572864 | tf_op jit(solution)/shard_map/all_to_all | solution.py:109
  568.7 40.2 %slice-start.9 = ((s8[6291456]{0:T(1024)(128)(4,1)}), s8[4194304]{0:T(1024)(128)(4,1)S(1)}, s32[]{:S(2)}) async-start(s8[6291456]{0:T(1024)(128)(4,1)} %bitcast.359), calls=%async_computation.31 | async-start | bytes 8388608
  571.6 37.3 %slice-start.10 = ((s8[6291456]{0:T(1024)(128)(4,1)}), s8[2097152]{0:T(1024)(128)(4,1)S(1)}, s32[]{:S(2)}) async-start(s8[6291456]{0:T(1024)(128)(4,1)} %bitcast.359), calls=%async_computation.32 | async-start | bytes 4194304
  573.6 45.7 %slice-start.6 = ((s8[9437184]{0:T(1024)(128)(4,1)}), s8[4194304]{0:T(1024)(128)(4,1)S(1)}, s32[]{:S(2)}) async-start(s8[9437184]{0:T(1024)(128)(4,1)} %bitcast.356), calls=%async_computation.28 | async-start | bytes 8388608
  574.9 12.1 %collective-permute-start.3 = (bf16[256,768]{1,0:T(8,128)(2,1)S(1)}, bf16[256,768]{1,0:T(8,128)(2,1)S(1)}, u32[]{:S(2)}, u32[]{:S(2)}) collective-permute-start(bf16[256,768]{1,0:T(8,128)(2,1)S(1)} %get-tuple-element.111), channel_id=1, source_target_pairs={{16,0},{17,1},{18,2},{19,3},{20,4},{21,5},{22,6},{23,7},{24,8},{25... | collective-permute-start | bytes 1179656 | tf_op jit(solution)/shard_map/ppermute | solution.py:19
  624.9 22.6 %all-to-all-start.11 = ((bf16[4,2,64,768]{3,2,1,0:T(8,128)(2,1)}), bf16[4,2,64,768]{3,2,1,0:T(8,128)(2,1)S(1)}, u32[]{:S(2)}, u32[]{:S(2)}) async-start(bf16[4,2,64,768]{3,2,1,0:T(8,128)(2,1)} %bitcast.346), calls=%async_computation.11 | async-start | bytes 1572864 | tf_op jit(solution)/shard_map/all_to_all | solution.py:109
  628.5 106.6 %reduce-scatter.4.cloned.1.call-start = ((), (), s32[]{:S(2)}) async-start(), calls=%async_computation.16 | async-start | bytes 6144000 | tf_op jit(solution)/shard_map/reduce_scatter | solution.py:325
  687.9 47.7 %copy-start.53 = (bf16[2,4,64,768]{3,2,1,0:T(8,128)(2,1)S(1)}, bf16[2,4,64,768]{3,2,1,0:T(8,128)(2,1)}, u32[]{:S(2)}) copy-start(bf16[2,4,64,768]{3,2,1,0:T(8,128)(2,1)} %copy.275) | copy-start | bytes 2359300
  687.9 47.7 %copy-start.55 = (bf16[2,4,64,768]{3,2,1,0:T(8,128)(2,1)S(1)}, bf16[2,4,64,768]{3,2,1,0:T(8,128)(2,1)}, u32[]{:S(2)}) copy-start(bf16[2,4,64,768]{3,2,1,0:T(8,128)(2,1)} %copy-done.54) | copy-start | bytes 2359300
  687.9 47.9 %copy-start.79 = (bf16[2,4,64,768]{3,2,1,0:T(8,128)(2,1)S(1)}, bf16[2,4,64,768]{3,2,1,0:T(8,128)(2,1)}, u32[]{:S(2)}) copy-start(bf16[2,4,64,768]{3,2,1,0:T(8,128)(2,1)} %copy-done.78) | copy-start | bytes 2359300
  687.9 107.4 %all-reduce.6.cloned.1.call-start = ((), (), s32[]{:S(2)}) async-start(), calls=%async_computation.17 | async-start | bytes 2457600 | tf_op jit(solution)/shard_map/psum | solution.py:339
  735.2 140.7 %reduce-scatter.8.cloned.1.call-start = ((), (), s32[]{:S(2)}) async-start(), calls=%async_computation.19 | async-start | bytes 11796480 | tf_op jit(solution)/shard_map/reduce_scatter | solution.py:325
  745.4 211.5 %reduce-scatter.6.cloned.1.call-start = ((), (), s32[]{:S(2)}) async-start(), calls=%async_computation.18 | async-start | bytes 11796480 | tf_op jit(solution)/shard_map/reduce_scatter | solution.py:325
  (161 other events, 1167.4 us)
Sparse Core Ops, SparseCore 0:
  14.0 41.2 all-gather.5
  56.9 64.2 all-gather.7
  122.7 64.2 all-gather.9
  688.1 47.0 reduce-scatter.3
  737.5 57.7 all-reduce.5
  797.8 78.0 reduce-scatter.7
  878.4 78.4 reduce-scatter.5

commit v2 on v1

--- a/solution.py
+++ b/solution.py
@@ -1,5 +1,6 @@
 import jax
 import jax.numpy as jnp
+import numpy as np
 from jax import lax
 from jax.experimental import pallas as pl
 from jax.experimental.pallas import tpu as pltpu
@@ -40,39 +41,44 @@
 
 def bucket_sums(grid_grads, buckets):
     head_count, length, _ = grid_grads.shape
-
-    def kernel(grads_ref, table_ref):
-        grid_values = bucket_grid_iota(length, buckets)
-        grads = grads_ref[0]
-        rows = [
-            jnp.sum(jnp.where(grid_values == number, grads, 0.0), axis=0, keepdims=True)
-            for number in range(buckets)
-        ]
-        table_ref[0] = jnp.concatenate(rows, axis=0)
+    high, wide = 8, 128
+    positions = np.arange(length)
+    offsets = positions[:, None] - positions[None, :]
+    known = np.where(offsets < 0, buckets // 2, 0)
+    for threshold in LIMITS:
+        known = known + (np.abs(offsets) >= threshold)
+
+    def kernel(grid_ref, grads_ref, table_ref):
+        sums = [None] * buckets
+        for top in range(0, length, high):
+            for left in range(0, length, wide):
+                block = (slice(top, top + high), slice(left, left + wide))
+                present = np.unique(known[block])
+                grads = grads_ref[(0,) + block]
+                named = grid_ref[block] if len(present) > 1 else None
+                for number in present.tolist():
+                    own = grads if named is None else jnp.where(named == number, grads, 0.0)
+                    sums[number] = own if sums[number] is None else sums[number] + own
+        empty = jnp.zeros((1, wide), jnp.float32)
+        table_ref[0] = jnp.concatenate(
+            [empty if own is None else jnp.sum(own, axis=0, keepdims=True) for own in sums], axis=0
+        )
 
     partial = pl.pallas_call(
         kernel,
         grid=(head_count,),
-        out_shape=jax.ShapeDtypeStruct((head_count, buckets, length), jnp.float32),
-        in_specs=[pl.BlockSpec((1, length, length), lambda h: (h, 0, 0))],
-        out_specs=pl.BlockSpec((1, buckets, length), lambda h: (h, 0, 0)),
+        out_shape=jax.ShapeDtypeStruct((head_count, buckets, wide), jnp.float32),
+        in_specs=[
+            pl.BlockSpec((length, length), lambda h: (0, 0)),
+            pl.BlockSpec((1, length, length), lambda h: (h, 0, 0)),
+        ],
+        out_specs=pl.BlockSpec((1, buckets, wide), lambda h: (h, 0, 0)),
         compiler_params=pltpu.CompilerParams(vmem_limit_bytes=16 * 1024 * 1024),
         cost_estimate=pl.CostEstimate(
-            flops=3 * buckets * grid_grads.size, bytes_accessed=5 * grid_grads.size, transcendentals=0
+            flops=30 * grid_grads.size, bytes_accessed=5 * grid_grads.size, transcendentals=0
         ),
-    )(grid_grads)
+    )(bucket_grid(length, buckets), grid_grads)
     return jnp.sum(partial, axis=-1).T
-
-
-def bucket_grid_iota(length, buckets):
-    offsets = lax.broadcasted_iota(jnp.int32, (length, length), 0) - lax.broadcasted_iota(
-        jnp.int32, (length, length), 1
-    )
-    distance = jnp.abs(offsets)
-    bucket = jnp.where(offsets < 0, buckets // 2, 0).astype(jnp.int32)
-    for threshold in LIMITS:
-        bucket = bucket + (distance >= threshold).astype(jnp.int32)
-    return bucket
 
 
 def root_scale(values):
@@ -86,6 +92,37 @@
         scaled * values, axis=-1, keepdims=True
     )
     return (grad_values, grad_gain)
+
+
+def from_partner(block, bit):
+    return lax.ppermute(block, "dp", [(i, i ^ bit) for i in range(lax.axis_size("dp"))])
+
+
+def gather_shards(near, far):
+    return jnp.concatenate([near, from_partner(near, 1), far, from_partner(far, 1)], axis=1)
+
+
+def half_grads(operands, grads, first):
+    width = operands.shape[2] // 4
+    return [
+        jnp.einsum(
+            "erf,erd->efd",
+            operands[:, :, k * width : (k + 1) * width],
+            grads,
+            preferred_element_type=jnp.float32,
+        ).astype(jnp.bfloat16)
+        for k in (first, first + 1)
+    ]
+
+
+def sum_shards(near, far):
+    wide = jnp.float32
+    passed = (far[0].astype(wide) + from_partner(far[1], 1).astype(wide)).astype(jnp.bfloat16)
+    return (
+        near[0].astype(wide)
+        + from_partner(near[1], 1).astype(wide)
+        + from_partner(passed, 2).astype(wide)
+    )
 
 
 def to_owners(outgoing, local_experts):
@@ -218,7 +255,7 @@
     return (result, stored)
 
 
-def layer_backward(grad_out, stored, mixer_set, position_bias, w_in_use, w_out_use):
+def layer_backward(grad_out, stored, mixer_set, position_bias, w_in_use, w_out_use, at_experts):
     gain_first, gain_second, w_project, w_output, w_router = mixer_set
     (
         hidden,
@@ -249,7 +286,11 @@
     grouped, before, activated = kept_rows
     grad_rows = to_owners(place(placement, grad_fetched), w_in_use.shape[0])
     grad_inputs, grad_before = expert_backward(grad_rows, before, w_in_use, w_out_use)
-    grad_routed = fetch(placement, to_tokens(grad_inputs))
+    kept_expert = dict(
+        grouped=grouped, activated=activated, grad_rows=grad_rows, grad_before=grad_before
+    )
+    grad_returned = at_experts(kept_expert, to_tokens(grad_inputs))
+    grad_routed = fetch(placement, grad_returned)
     grad_logits = (
         (gate_value * grad_gate)[:, None] * (chosen.astype(jnp.float32) - router)
     ).astype(jnp.bfloat16)
@@ -316,9 +357,7 @@
         routed=routed,
         grad_logits=grad_logits,
     )
-    return (grad_hidden, kept, dict(
-        grouped=grouped, activated=activated, grad_rows=grad_rows, grad_before=grad_before
-    ))
+    return (grad_hidden, kept)
 
 
 def scatter_sum(full, axis):
@@ -389,8 +428,11 @@
     small = pack_small([w_router[0], gains], bias_table[0], 1)
     packed = jnp.concatenate([w_query[0], w_key[0], w_value[0], w_output[0], small], axis=1)
     packed = lax.all_gather(packed, "dp", axis=0, tiled=True)
-    w_in_use = lax.all_gather(expert_in[0], "dp", axis=1, tiled=True)
-    w_out_use = lax.all_gather(expert_out[0], "dp", axis=1, tiled=True)
+    far_in = from_partner(expert_in[0], 2)
+    far_in, near_out = lax.optimization_barrier((far_in, expert_out[0]))
+    far_out = from_partner(near_out, 2)
+    w_in_use = gather_shards(expert_in[0], far_in)
+    w_out_use = gather_shards(expert_out[0], far_out)
     buckets = bias_table.shape[1] * shards
     router_full, gains, bias_rows = unpack_small(
         packed[:, 4 * model_width :],
@@ -436,48 +478,47 @@
     returning = jnp.zeros((SEQ, model_width), jnp.bfloat16)
     mixer_kept = []
     expert_kept = []
+    expert_sum = []
+
+    def real(kept, name):
+        return (kept[1][name], jnp.where(is_first, kept[2][name], kept[0][name]))
+
+    def at_experts(kept, returned):
+        expert_kept.append(kept)
+        if len(expert_kept) <= MICRO:
+            return returned
+        rows = {name: jnp.concatenate(real(expert_kept, name), axis=1) for name in kept}
+        halves = [
+            half_grads(rows[operand], rows[grads], first)
+            for operand, grads in (("activated", "grad_rows"), ("grad_before", "grouped"))
+            for first in (2, 0)
+        ]
+        returned, halves = lax.optimization_barrier((returned, halves))
+        far_out, near_out, far_in, near_in = halves
+        expert_sum.extend([sum_shards(near_in, far_in), sum_shards(near_out, far_out)])
+        return returned
+
     for step_number in range(MICRO + 1):
         if step_number < MICRO:
             cotangent = block_rows(local_rows, MICRO - 1 - step_number).astype(jnp.float32)
         else:
             cotangent = jnp.zeros((SEQ, model_width), jnp.float32)
         grad_out = jnp.where(is_first, returning.astype(jnp.float32), cotangent)
-        grad_hidden, kept_mixer, kept_expert = layer_backward(
+        grad_hidden, kept_mixer = layer_backward(
             grad_out,
             stored_list[MICRO - step_number],
             mixer_set,
             position_bias,
             w_in_use,
             w_out_use,
+            at_experts,
         )
         if step_number < MICRO:
             returning = from_behind(grad_hidden.astype(jnp.bfloat16), "section", -1)
         if step_number >= 1:
             input_grads[MICRO - step_number] = grad_hidden
         mixer_kept.append(kept_mixer)
-        expert_kept.append(kept_expert)
-
-    def real(kept, name):
-        return (kept[1][name], jnp.where(is_first, kept[2][name], kept[0][name]))
-
-    experts_rows = {
-        name: jnp.concatenate(real(expert_kept, name), axis=1) for name in expert_kept[0]
-    }
-    grad_out_full = jnp.einsum(
-        "erf,erd->efd",
-        experts_rows["activated"],
-        experts_rows["grad_rows"],
-        preferred_element_type=jnp.float32,
-    )
-    grad_w_out = scatter_sum(grad_out_full.astype(jnp.bfloat16), 1).astype(jnp.float32)
-    grad_in_full = jnp.einsum(
-        "erf,erd->efd",
-        experts_rows["grad_before"],
-        experts_rows["grouped"],
-        preferred_element_type=jnp.float32,
-    )
-    grad_w_in = scatter_sum(grad_in_full.astype(jnp.bfloat16), 1).astype(jnp.float32)
-    expert_sum = (grad_w_in, grad_w_out)
+
     summed = ("gains", "grad_scores")
     sums = {
         name: sum(part.astype(jnp.float32) for part in real(mixer_kept, name)) for name in summed

time: 980 us -> 880 us (0.90)
  waiting for transfers between devices: 460 us -> 365 us
  blocking collectives: 88.8 us -> 42.7 us
  other arithmetic: 77.1 us -> 109 us
  starting transfers between devices: 45.9 us -> 63.1 us
    ppermute x0 -> x12, waiting for transfers between devices: none -> 161 us  [from_partner(): lax.ppermute(block, 'dp', [(i, i ^ bit) for i in range(lax.axis_size('dp'...]
    reduce_scatter x3 -> x1, waiting for transfers between devices: 199 us -> 61.6 us  [scatter_sum(): return lax.psum_scatter(full, 'dp', scatter_dimension=axis, tiled=True)]
    all_gather x2 -> x0, waiting for transfers between devices: 69.7 us -> none  [the longest x1 54.2 us: local(): w_out_use = lax.all_gather(expert_out[0], 'dp', axis=1, tiled=True)]
    all_to_all x4 -> x2, blocking collectives: 88.8 us -> 42.7 us  [to_owners(): lax.all_to_all(outgoing.reshape(owners, local_experts, capacity, model_wi...]
    psum x1, waiting for transfers between devices: 34.6 us -> 0.01 us  [reduce_mixer(): total = lax.psum(scatter_sum(packed, 0), 'expert').astype(jnp.float32)]
    all_gather x1, waiting for transfers between devices: 21.4 us -> 0.01 us  [local(): packed = lax.all_gather(packed, 'dp', axis=0, tiled=True)]
    concatenate x0 -> x2, other arithmetic: none -> 17.3 us  [gather_shards(): jnp.concatenate([near, from_partner(near, 1), far, from_partner(far, 1)],...]
    all_to_all x2 -> x4, waiting for transfers between devices: 30.2 us -> 41.7 us  [to_owners(): lax.all_to_all(outgoing.reshape(owners, local_experts, capacity, model_wi...]
  transfers between devices with their start and end apart: 19 -> 29, of which waited for: 19 -> 21; matrix products, arithmetic and copies ran while one was open for 14% -> 19% of each run, Pallas kernels for 0% -> 0%
where the time goes in v2:
time: 880 us; the launch traced here: 864 us
  waiting for transfers between devices  365 us (41%)
  matrix products  198 us (22%)
  other arithmetic  109 us (12%)
  local copies, waits for them, and re-layouts  64.3 us (7%)
  starting transfers between devices  63.1 us (7%)
  blocking collectives  42.7 us (5%)
  between operations  16.7 us (2%)
    ppermute x12, waiting for transfers between devices, from_partner(): lax.ppermute(block, 'dp', [(i, i ^ bit) for i in range(lax.axis_size('dp'...  161 us
    all_to_all x6, waiting for transfers between devices, to_tokens(): lax.all_to_all(produced.reshape(local_experts, owners, capacity, model_wi...  69 us
    reduce_scatter x1, waiting for transfers between devices, scatter_sum(): return lax.psum_scatter(full, 'dp', scatter_dimension=axis, tiled=True)  61.6 us
    all_to_all x2, blocking collectives, to_owners(): lax.all_to_all(outgoing.reshape(owners, local_experts, capacity, model_wi...  42.7 us
    all_to_all x4, waiting for transfers between devices, to_owners(): lax.all_to_all(outgoing.reshape(owners, local_experts, capacity, model_wi...  41.7 us
    dot_general x3, matrix products, expert_backward(): jnp.einsum('erd,efd->erf', grad_rows, w_out_use, preferred_element_type=j...  32.3 us
    ppermute x4, waiting for transfers between devices, from_behind(): return lax.ppermute(block, axis, route)  31.4 us
    all_to_all x6, starting transfers between devices, to_tokens(): lax.all_to_all(produced.reshape(local_experts, owners, capacity, model_wi...  25.4 us
  transfers between devices with their start and end apart: 29, of which 21 were waited for; matrix products, arithmetic and copies ran while one was open for 19% of the time, Pallas kernels for 0%

profile of v2, /device:TPU:0, one launch (start us, length us, event | category | flops | bytes accessed | tf_op | source)
XLA Modules:
  0.0 864.0 jit_solution(3049482412824434830)
XLA Ops:
  30.5 64.4 %collective-permute-done.1 = bf16[2,768,768]{2,1,0:T(8,128)(2,1)} collective-permute-done((bf16[2,768,768]{2,1,0:T(8,128)(2,1)}, bf16[2,768,768]{2,1,0:T(8,128)(2,1)}, u32[]{:S(2)}, u32[]{:S(2)}) %collective-permute-start.1) | collective-permute-done | bytes 2359328 | tf_op jit(solution)/shard_map/ppermute | solution.py:98
  110.3 37.4 %collective-permute-done.4 = bf16[2,768,768]{2,1,0:T(8,128)(2,1)} collective-permute-done((bf16[2,768,768]{2,1,0:T(8,128)(2,1)}, bf16[2,768,768]{2,1,0:T(8,128)(2,1)}, u32[]{:S(2)}, u32[]{:S(2)}) %collective-permute-start.4) | collective-permute-done | bytes 2359328 | tf_op jit(solution)/shard_map/ppermute | solution.py:98
  148.9 13.1 %select_select_fusion = f32[12,256,256]{2,1,0:T(8,128)S(1)} fusion(f32[12]{0:T(128)S(1)} %get-tuple-element.148, f32[12]{0:T(128)S(1)} %get-tuple-element.149, f32[12]{0:T(128)S(1)} %get-tuple-element.150, f32[12]{0:T(128)S(1)} %get-tuple-element.151, f32[12]{0:T(128)S(1)} %get-tuple-element.152, f32[12]{0:T(128)S(1)} %get-tuple-element.153, ...), kind=kLoop, calls=%fused_computation.68 | loop fusion | flops 24379392 | bytes 5178880 | tf_op jit(solution)/shard_map/jit(_where)/select_n | solution.py:38
  183.5 8.7 %pad_maximum_fusion = bf16[2,3072,768]{2,1,0:T(8,128)(2,1)} fusion(bf16[2,768,768]{2,1,0:T(8,128)(2,1)} %collective-permute-done.2, bf16[2,768,768]{2,1,0:T(8,128)(2,1)} %collective-permute-done.1, bf16[2,768,768]{2,1,0:T(8,128)(2,1)} %collective-permute-done, bf16[2,768,768]{2,1,0:T(8,128)(2,1)} %bitcast.55), kind=kLoop, calls=%fused_computation | loop fusion | flops 37748736 | bytes 18874368 | tf_op jit(solution)/shard_map/concatenate | solution.py:102
  192.2 8.6 pad_maximum_fusion.1
  204.3 5.6 fusion.250
  219.8 18.6 %all-to-all-done.1 = bf16[4,2,64,768]{3,2,1,0:T(8,128)(2,1)S(1)} async-done(((bf16[4,2,64,768]{3,2,1,0:T(8,128)(2,1)}), bf16[4,2,64,768]{3,2,1,0:T(8,128)(2,1)S(1)}, u32[]{:S(2)}, u32[]{:S(2)}) %all-to-all-start.1) | async-done | bytes 786464 | tf_op jit(solution)/shard_map/all_to_all | solution.py:146
  244.1 6.6 collective-permute-done.6
  265.3 21.1 %all_to_all.60 = bf16[4,2,64,768]{3,2,1,0:T(8,128)(2,1)S(1)} all-to-all(bf16[4,2,64,768]{3,2,1,0:T(8,128)(2,1)S(1)} %bitcast.398), channel_id=1, replica_groups=mesh['section'=2,'expert'=4,'dp'=4] {'expert'}, dimensions={0} | all-to-all | bytes 1572864 | tf_op jit(solution)/shard_map/all_to_all | solution.py:132
  286.5 5.2 multiply_convert_fusion.1
  291.7 7.5 convolution_convert_fusion.21
  308.0 15.3 %all-to-all-done.3 = bf16[4,2,64,768]{3,2,1,0:T(8,128)(2,1)} async-done(((bf16[4,2,64,768]{3,2,1,0:T(8,128)(2,1)}), bf16[4,2,64,768]{3,2,1,0:T(8,128)(2,1)}, u32[]{:S(2)}, u32[]{:S(2)}) %all-to-all-start.3) | async-done | bytes 786464 | tf_op jit(solution)/shard_map/all_to_all | solution.py:146
  330.7 7.3 collective-permute-done.7
  373.6 12.7 %all-to-all-done.5 = bf16[4,2,64,768]{3,2,1,0:T(8,128)(2,1)} async-done(((bf16[4,2,64,768]{3,2,1,0:T(8,128)(2,1)}), bf16[4,2,64,768]{3,2,1,0:T(8,128)(2,1)}, u32[]{:S(2)}, u32[]{:S(2)}) %all-to-all-start.5) | async-done | bytes 786464 | tf_op jit(solution)/shard_map/all_to_all | solution.py:132
  392.6 17.6 %all-to-all-done.4 = bf16[4,2,64,768]{3,2,1,0:T(8,128)(2,1)} async-done(((bf16[4,2,64,768]{3,2,1,0:T(8,128)(2,1)}), bf16[4,2,64,768]{3,2,1,0:T(8,128)(2,1)}, u32[]{:S(2)}, u32[]{:S(2)}) %all-to-all-start.4) | async-done | bytes 786464 | tf_op jit(solution)/shard_map/all_to_all | solution.py:132
  412.3 5.5 fusion.251
  417.7 9.1 %convolution_convert_fusion.17 = bf16[2,256,768]{2,1,0:T(8,128)(2,1)S(1)} fusion(bf16[2,3072,768]{2,1,0:T(8,128)(2,1)} %pad_maximum_fusion.1, f32[2,256,3072]{2,1,0:T(8,128)S(1)} %fusion.251), kind=kOutput, calls=%fused_computation.132 | convolution fusion | flops 2430468096 | bytes 16515072 | tf_op jit(solution)/shard_map/erf,efd->erd/dot_general | solution.py:159
  432.4 8.9 %fusion.20 = bf16[2,256,3072]{2,1,0:T(8,128)(2,1)S(1)} fusion(f32[2,256,3072]{2,1,0:T(8,128)} %copy-done.54, bf16[2,256,768]{2,1,0:T(8,128)(2,1)} %bitcast.364, bf16[2,3072,768]{2,1,0:T(8,128)(2,1)} %pad_maximum_fusion.1), kind=kOutput, calls=%fused_computation.40 | convolution fusion | flops 2447376384 | bytes 19660800 | tf_op jit(solution)/shard_map/erd,efd->erf/dot_general | solution.py:164
  441.3 7.5 convolution_convert_fusion.18
  462.1 13.8 %all-to-all-done.6 = bf16[4,2,64,768]{3,2,1,0:T(8,128)(2,1)} async-done(((bf16[4,2,64,768]{3,2,1,0:T(8,128)(2,1)}), bf16[4,2,64,768]{3,2,1,0:T(8,128)(2,1)}, u32[]{:S(2)}, u32[]{:S(2)}) %all-to-all-start.6) | async-done | bytes 786464 | tf_op jit(solution)/shard_map/all_to_all | solution.py:146
  495.8 10.8 %collective-permute-done.8 = bf16[256,768]{1,0:T(8,128)(2,1)S(1)} collective-permute-done((bf16[256,768]{1,0:T(8,128)(2,1)S(1)}, bf16[256,768]{1,0:T(8,128)(2,1)S(1)}, u32[]{:S(2)}, u32[]{:S(2)}) %collective-permute-start.8) | collective-permute-done | bytes 393248 | tf_op jit(solution)/shard_map/ppermute | solution.py:20
  507.1 21.6 %all_to_all.61 = bf16[4,2,64,768]{3,2,1,0:T(8,128)(2,1)S(1)} all-to-all(bf16[4,2,64,768]{3,2,1,0:T(8,128)(2,1)S(1)} %bitcast.402), channel_id=1, replica_groups=mesh['section'=2,'expert'=4,'dp'=4] {'expert'}, dimensions={0} | all-to-all | bytes 1572864 | tf_op jit(solution)/shard_map/all_to_all | solution.py:132
  528.9 9.0 %fusion.13 = bf16[2,256,3072]{2,1,0:T(8,128)(2,1)S(1)} fusion(f32[2,256,3072]{2,1,0:T(8,128)} %get-tuple-element.194, bf16[2,256,768]{2,1,0:T(8,128)(2,1)S(1)} %bitcast.325, bf16[2,3072,768]{2,1,0:T(8,128)(2,1)} %pad_maximum_fusion.1), kind=kOutput, calls=%fused_computation.33 | convolution fusion | flops 2447376384 | bytes 19660800 | tf_op jit(solution)/shard_map/erd,efd->erf/dot_general | solution.py:164
  549.3 15.6 %all-to-all-done.9 = bf16[4,2,64,768]{3,2,1,0:T(8,128)(2,1)} async-done(((bf16[4,2,64,768]{3,2,1,0:T(8,128)(2,1)}), bf16[4,2,64,768]{3,2,1,0:T(8,128)(2,1)}, u32[]{:S(2)}, u32[]{:S(2)}) %all-to-all-start.9) | async-done | bytes 786464 | tf_op jit(solution)/shard_map/all_to_all | solution.py:146
  590.6 6.7 collective-permute-done.9
  613.8 8.0 all-to-all-done.10
  624.2 14.5 %broadcast_select_fusion = (bf16[2,256,3072]{2,1,0:T(8,128)(2,1)S(1)}, bf16[2,256,3072]{2,1,0:T(8,128)(2,1)}, bf16[2,256,3072]{2,1,0:T(8,128)(2,1)}) fusion(bf16[2,256,3072]{2,1,0:T(8,128)(2,1)} %copy-done.180, pred[]{:T(512)S(6)} %eq.378, f32[2,256,3072]{2,1,0:T(8,128)} %copy-done.53, f32[2,256,3072]{2,1,0:T(8,128)} %copy-done.54, ...), kind=kOutput, calls=%fused_computation.70 | convolution fusion | flops 2467823616 | bytes 35389440 | tf_op jit(solution)/shard_map/erd,efd->erf/dot_general | solution.py:164
  726.2 61.6 %reduce-scatter.2.cloned.1.call-done = bf16[192,3200]{1,0:T(8,128)(2,1)} async-done(((bf16[768,3200]{1,0:T(8,128)(2,1)}), bf16[192,3200]{1,0:T(8,128)(2,1)}) %reduce-scatter.2.cloned.1.call-update) | async-done | bytes 1228816 | tf_op jit(solution)/shard_map/reduce_scatter | solution.py:364
  790.8 6.2 collective-permute-done.12
  797.0 5.5 add_bitcast_fusion.1
  802.5 44.3 %collective-permute-done.15 = bf16[2,768,768]{2,1,0:T(8,128)(2,1)} collective-permute-done((bf16[2,768,768]{2,1,0:T(8,128)(2,1)}, bf16[2,768,768]{2,1,0:T(8,128)(2,1)}, u32[]{:S(2)}, u32[]{:S(2)}) %collective-permute-start.15) | collective-permute-done | bytes 2359328 | tf_op jit(solution)/shard_map/ppermute | solution.py:98
  846.8 5.5 add_bitcast_fusion
  (677 shorter events, 343.8 us)
Async XLA Ops:
  7.2 101.7 %copy-start.31 = (bf16[1,512,768]{2,1,0:T(8,128)(2,1)S(1)}, bf16[1,512,768]{2,1,0:T(8,128)(2,1)}, u32[]{:S(2)}) copy-start(bf16[1,512,768]{2,1,0:T(8,128)(2,1)} %param.12) | copy-start | bytes 2359300
  7.2 140.5 %all-gather.2.cloned.1.call-start = ((), (), s32[]{:S(2)}) async-start(), calls=%async_computation.13 | async-start | bytes 6144000 | tf_op jit(solution)/shard_map/all_gather | solution.py:430
  14.0 80.9 %collective-permute-start.1 = (bf16[2,768,768]{2,1,0:T(8,128)(2,1)}, bf16[2,768,768]{2,1,0:T(8,128)(2,1)}, u32[]{:S(2)}, u32[]{:S(2)}) collective-permute-start(bf16[2,768,768]{2,1,0:T(8,128)(2,1)} %bitcast.55), channel_id=1, source_target_pairs={{0,2},{1,3},{2,0},{3,1},{4,6},{5,7},{6,4},{7,5},{8,10},{9,11},{10,... | collective-permute-start | bytes 7077896 | tf_op jit(solution)/shard_map/ppermute | solution.py:98
  17.0 166.4 %collective-permute-start = (bf16[2,768,768]{2,1,0:T(8,128)(2,1)}, bf16[2,768,768]{2,1,0:T(8,128)(2,1)}, u32[]{:S(2)}, u32[]{:S(2)}) collective-permute-start(bf16[2,768,768]{2,1,0:T(8,128)(2,1)} %bitcast.55), channel_id=1, source_target_pairs={{0,1},{1,0},{2,3},{3,2},{4,5},{5,4},{6,7},{7,6},{8,9},{9,8},{10,11... | collective-permute-start | bytes 7077896 | tf_op jit(solution)/shard_map/ppermute | solution.py:98
  17.0 175.2 %collective-permute-start.3 = (bf16[2,768,768]{2,1,0:T(8,128)(2,1)}, bf16[2,768,768]{2,1,0:T(8,128)(2,1)}, u32[]{:S(2)}, u32[]{:S(2)}) collective-permute-start(bf16[2,768,768]{2,1,0:T(8,128)(2,1)} %bitcast.56), channel_id=1, source_target_pairs={{0,1},{1,0},{2,3},{3,2},{4,5},{5,4},{6,7},{7,6},{8,9},{9,8},{10,11... | collective-permute-start | bytes 7077896 | tf_op jit(solution)/shard_map/ppermute | solution.py:98
  94.9 52.7 %collective-permute-start.4 = (bf16[2,768,768]{2,1,0:T(8,128)(2,1)}, bf16[2,768,768]{2,1,0:T(8,128)(2,1)}, u32[]{:S(2)}, u32[]{:S(2)}) collective-permute-start(bf16[2,768,768]{2,1,0:T(8,128)(2,1)} %bitcast.56), channel_id=1, source_target_pairs={{0,2},{1,3},{2,0},{3,1},{4,6},{5,7},{6,4},{7,5},{8,10},{9,11},{10,... | collective-permute-start | bytes 7077896 | tf_op jit(solution)/shard_map/ppermute | solution.py:98
  108.7 111.0 %copy-start.131 = (s32[1,256,1]{1,2,0:T(1,128)}, s32[1,256,1]{1,2,0:T(1,128)S(1)}, u32[]{:S(2)}) copy-start(s32[1,256,1]{1,2,0:T(1,128)S(1)} %get-tuple-element.180) | copy-start | bytes 3076
  108.7 134.8 %copy-start.129 = (s32[1,256,1]{1,2,0:T(1,128)}, s32[1,256,1]{1,2,0:T(1,128)S(1)}, u32[]{:S(2)}) copy-start(s32[1,256,1]{1,2,0:T(1,128)S(1)} %get-tuple-element.179) | copy-start | bytes 3076
  110.2 73.2 %collective-permute-start.2 = (bf16[2,768,768]{2,1,0:T(8,128)(2,1)}, bf16[2,768,768]{2,1,0:T(8,128)(2,1)}, u32[]{:S(2)}, u32[]{:S(2)}) collective-permute-start(bf16[2,768,768]{2,1,0:T(8,128)(2,1)} %collective-permute-done.1), channel_id=1, source_target_pairs={{0,1},{1,0},{2,3},{3,2},{4,5},{5,4},{6,7},{7,6},{8,9},{9,8},{10,11... | collective-permute-start | bytes 7077896 | tf_op jit(solution)/shard_map/ppermute | solution.py:98
  147.7 44.5 %collective-permute-start.5 = (bf16[2,768,768]{2,1,0:T(8,128)(2,1)}, bf16[2,768,768]{2,1,0:T(8,128)(2,1)}, u32[]{:S(2)}, u32[]{:S(2)}) collective-permute-start(bf16[2,768,768]{2,1,0:T(8,128)(2,1)} %collective-permute-done.4), channel_id=1, source_target_pairs={{0,1},{1,0},{2,3},{3,2},{4,5},{5,4},{6,7},{7,6},{8,9},{9,8},{10,11... | collective-permute-start | bytes 7077896 | tf_op jit(solution)/shard_map/ppermute | solution.py:98
  178.7 25.6 %all-to-all-start = ((bf16[4,2,64,768]{3,2,1,0:T(8,128)(2,1)}), bf16[4,2,64,768]{3,2,1,0:T(8,128)(2,1)S(1)}, u32[]{:S(2)}, u32[]{:S(2)}) async-start(bf16[4,2,64,768]{3,2,1,0:T(8,128)(2,1)} %bitcast.52), calls=%async_computation | async-start | bytes 1572864 | tf_op jit(solution)/shard_map/all_to_all | solution.py:132
  215.0 23.4 %all-to-all-start.1 = ((bf16[4,2,64,768]{3,2,1,0:T(8,128)(2,1)}), bf16[4,2,64,768]{3,2,1,0:T(8,128)(2,1)S(1)}, u32[]{:S(2)}, u32[]{:S(2)}) async-start(bf16[4,2,64,768]{3,2,1,0:T(8,128)(2,1)} %bitcast.313), calls=%async_computation.1 | async-start | bytes 1572864 | tf_op jit(solution)/shard_map/all_to_all | solution.py:146
  239.7 11.0 %collective-permute-start.6 = (bf16[256,768]{1,0:T(8,128)(2,1)S(1)}, bf16[256,768]{1,0:T(8,128)(2,1)S(1)}, u32[]{:S(2)}, u32[]{:S(2)}) collective-permute-start(bf16[256,768]{1,0:T(8,128)(2,1)S(1)} %get-tuple-element.187), channel_id=1, source_target_pairs={{0,16},{1,17},{2,18},{3,19},{4,20},{5,21},{6,22},{7,23},{8,24},{9,... | collective-permute-start | bytes 1179656 | tf_op jit(solution)/shard_map/ppermute | solution.py:20
  300.1 23.2 %all-to-all-start.3 = ((bf16[4,2,64,768]{3,2,1,0:T(8,128)(2,1)}), bf16[4,2,64,768]{3,2,1,0:T(8,128)(2,1)}, u32[]{:S(2)}, u32[]{:S(2)}) async-start(bf16[4,2,64,768]{3,2,1,0:T(8,128)(2,1)} %bitcast.370), calls=%async_computation.3 | async-start | bytes 1572864 | tf_op jit(solution)/shard_map/all_to_all | solution.py:146
  326.1 12.0 %collective-permute-start.7 = (bf16[256,768]{1,0:T(8,128)(2,1)S(1)}, bf16[256,768]{1,0:T(8,128)(2,1)S(1)}, u32[]{:S(2)}, u32[]{:S(2)}) collective-permute-start(bf16[256,768]{1,0:T(8,128)(2,1)S(1)} %get-tuple-element.197), channel_id=1, source_target_pairs={{0,16},{1,17},{2,18},{3,19},{4,20},{5,21},{6,22},{7,23},{8,24},{9,... | collective-permute-start | bytes 1179656 | tf_op jit(solution)/shard_map/ppermute | solution.py:20
  363.4 22.9 %all-to-all-start.5 = ((bf16[4,2,64,768]{3,2,1,0:T(8,128)(2,1)}), bf16[4,2,64,768]{3,2,1,0:T(8,128)(2,1)}, u32[]{:S(2)}, u32[]{:S(2)}) async-start(bf16[4,2,64,768]{3,2,1,0:T(8,128)(2,1)} %bitcast.375), calls=%async_computation.5 | async-start | bytes 1572864 | tf_op jit(solution)/shard_map/all_to_all | solution.py:132
  386.3 23.9 %all-to-all-start.4 = ((bf16[4,2,64,768]{3,2,1,0:T(8,128)(2,1)}), bf16[4,2,64,768]{3,2,1,0:T(8,128)(2,1)}, u32[]{:S(2)}, u32[]{:S(2)}) async-start(bf16[4,2,64,768]{3,2,1,0:T(8,128)(2,1)} %bitcast.395), calls=%async_computation.4 | async-start | bytes 1572864 | tf_op jit(solution)/shard_map/all_to_all | solution.py:132
  427.8 24.3 %all-to-all-start.7 = ((bf16[4,2,64,768]{3,2,1,0:T(8,128)(2,1)}), bf16[4,2,64,768]{3,2,1,0:T(8,128)(2,1)}, u32[]{:S(2)}, u32[]{:S(2)}) async-start(bf16[4,2,64,768]{3,2,1,0:T(8,128)(2,1)} %bitcast.371), calls=%async_computation.7 | async-start | bytes 1572864 | tf_op jit(solution)/shard_map/all_to_all | solution.py:146
  452.1 23.9 %all-to-all-start.6 = ((bf16[4,2,64,768]{3,2,1,0:T(8,128)(2,1)}), bf16[4,2,64,768]{3,2,1,0:T(8,128)(2,1)}, u32[]{:S(2)}, u32[]{:S(2)}) async-start(bf16[4,2,64,768]{3,2,1,0:T(8,128)(2,1)} %bitcast.368), calls=%async_computation.6 | async-start | bytes 1572864 | tf_op jit(solution)/shard_map/all_to_all | solution.py:146
  494.5 12.1 %collective-permute-start.8 = (bf16[256,768]{1,0:T(8,128)(2,1)S(1)}, bf16[256,768]{1,0:T(8,128)(2,1)S(1)}, u32[]{:S(2)}, u32[]{:S(2)}) collective-permute-start(bf16[256,768]{1,0:T(8,128)(2,1)S(1)} %fusion.84), channel_id=1, source_target_pairs={{16,0},{17,1},{18,2},{19,3},{20,4},{21,5},{22,6},{23,7},{24,8},{25... | collective-permute-start | bytes 1179656 | tf_op jit(solution)/shard_map/ppermute | solution.py:20
  541.5 23.3 %all-to-all-start.9 = ((bf16[4,2,64,768]{3,2,1,0:T(8,128)(2,1)}), bf16[4,2,64,768]{3,2,1,0:T(8,128)(2,1)}, u32[]{:S(2)}, u32[]{:S(2)}) async-start(bf16[4,2,64,768]{3,2,1,0:T(8,128)(2,1)} %bitcast.369), calls=%async_computation.9 | async-start | bytes 1572864 | tf_op jit(solution)/shard_map/all_to_all | solution.py:146
  585.0 12.3 %collective-permute-start.9 = (bf16[256,768]{1,0:T(8,128)(2,1)}, bf16[256,768]{1,0:T(8,128)(2,1)S(1)}, u32[]{:S(2)}, u32[]{:S(2)}) collective-permute-start(bf16[256,768]{1,0:T(8,128)(2,1)} %get-tuple-element.136), channel_id=1, source_target_pairs={{16,0},{17,1},{18,2},{19,3},{20,4},{21,5},{22,6},{23,7},{24,8},{25... | collective-permute-start | bytes 1179656 | tf_op jit(solution)/shard_map/ppermute | solution.py:20
  598.7 23.2 %all-to-all-start.10 = ((bf16[4,2,64,768]{3,2,1,0:T(8,128)(2,1)}), bf16[4,2,64,768]{3,2,1,0:T(8,128)(2,1)}, u32[]{:S(2)}, u32[]{:S(2)}) async-start(bf16[4,2,64,768]{3,2,1,0:T(8,128)(2,1)} %bitcast.394), calls=%async_computation.10 | async-start | bytes 1572864 | tf_op jit(solution)/shard_map/all_to_all | solution.py:132
  651.1 24.4 %all-to-all-start.11 = ((bf16[4,2,64,768]{3,2,1,0:T(8,128)(2,1)}), bf16[4,2,64,768]{3,2,1,0:T(8,128)(2,1)}, u32[]{:S(2)}, u32[]{:S(2)}) async-start(bf16[4,2,64,768]{3,2,1,0:T(8,128)(2,1)} %bitcast.367), calls=%async_computation.11 | async-start | bytes 1572864 | tf_op jit(solution)/shard_map/all_to_all | solution.py:146
  655.9 131.9 %reduce-scatter.2.cloned.1.call-start = ((), (), s32[]{:S(2)}) async-start(), calls=%async_computation.14 | async-start | bytes 6144000 | tf_op jit(solution)/shard_map/reduce_scatter | solution.py:364
  707.7 144.6 %all-reduce.6.cloned.1.call-start = ((), (), s32[]{:S(2)}) async-start(), calls=%async_computation.15 | async-start | bytes 2457600 | tf_op jit(solution)/shard_map/psum | solution.py:378
  707.7 4.8 collective-permute-start.11
  707.8 14.9 %collective-permute-start.14 = (bf16[2,768,768]{2,1,0:T(8,128)(2,1)}, bf16[2,768,768]{2,1,0:T(8,128)(2,1)S(1)}, u32[]{:S(2)}, u32[]{:S(2)}) collective-permute-start(bf16[2,768,768]{2,1,0:T(8,128)(2,1)} %convolution_convert_fusion.10), channel_id=1, source_target_pairs={{0,1},{1,0},{2,3},{3,2},{4,5},{5,4},{6,7},{7,6},{8,9},{9,8},{10,11... | collective-permute-start | bytes 7077896 | tf_op jit(solution)/shard_map/ppermute | solution.py:98
  708.3 82.5 %collective-permute-start.10 = (bf16[2,768,768]{2,1,0:T(8,128)(2,1)}, bf16[2,768,768]{2,1,0:T(8,128)(2,1)}, u32[]{:S(2)}, u32[]{:S(2)}) collective-permute-start(bf16[2,768,768]{2,1,0:T(8,128)(2,1)} %convolution_convert_fusion.4), channel_id=1, source_target_pairs={{0,1},{1,0},{2,3},{3,2},{4,5},{5,4},{6,7},{7,6},{8,9},{9,8},{10,11... | collective-permute-start | bytes 7077896 | tf_op jit(solution)/shard_map/ppermute | solution.py:98
  716.2 80.8 %collective-permute-start.12 = (bf16[2,768,768]{2,1,0:T(8,128)(2,1)}, bf16[2,768,768]{2,1,0:T(8,128)(2,1)}, u32[]{:S(2)}, u32[]{:S(2)}) collective-permute-start(bf16[2,768,768]{2,1,0:T(8,128)(2,1)} %add_convert_fusion.1), channel_id=1, source_target_pairs={{0,2},{1,3},{2,0},{3,1},{4,6},{5,7},{6,4},{7,5},{8,10},{9,11},{10,... | collective-permute-start | bytes 7077896 | tf_op jit(solution)/shard_map/ppermute | solution.py:98
  717.8 84.7 %collective-permute-start.13 = (bf16[2,768,768]{2,1,0:T(8,128)(2,1)}, bf16[2,768,768]{2,1,0:T(8,128)(2,1)}, u32[]{:S(2)}, u32[]{:S(2)}) collective-permute-start(bf16[2,768,768]{2,1,0:T(8,128)(2,1)} %convolution_convert_fusion.8), channel_id=1, source_target_pairs={{0,1},{1,0},{2,3},{3,2},{4,5},{5,4},{6,7},{7,6},{8,9},{9,8},{10,11... | collective-permute-start | bytes 7077896 | tf_op jit(solution)/shard_map/ppermute | solution.py:98
  724.7 122.1 %collective-permute-start.15 = (bf16[2,768,768]{2,1,0:T(8,128)(2,1)}, bf16[2,768,768]{2,1,0:T(8,128)(2,1)}, u32[]{:S(2)}, u32[]{:S(2)}) collective-permute-start(bf16[2,768,768]{2,1,0:T(8,128)(2,1)} %add_convert_fusion), channel_id=1, source_target_pairs={{0,2},{1,3},{2,0},{3,1},{4,6},{5,7},{6,4},{7,5},{8,10},{9,11},{10,... | collective-permute-start | bytes 7077896 | tf_op jit(solution)/shard_map/ppermute | solution.py:98
  (197 other events, 1869.2 us)
Sparse Core Ops, SparseCore 0:
  14.1 67.7 all-gather.1
  707.8 79.9 reduce-scatter.1
  790.3 57.7 all-reduce.5

commit v3 on v2

--- a/solution.py
+++ b/solution.py
@@ -30,23 +30,56 @@
     return bucket
 
 
-def bias_of(bias_rows, length):
-    buckets = bias_rows.shape[0]
-    grid_values = bucket_grid(length, buckets)[None]
-    bias = jnp.broadcast_to(bias_rows[0][:, None, None], (bias_rows.shape[1], length, length))
-    for number in range(1, buckets):
-        bias = jnp.where(grid_values == number, bias_rows[number][:, None, None], bias)
-    return bias
-
-
-def bucket_sums(grid_grads, buckets):
-    head_count, length, _ = grid_grads.shape
-    high, wide = 8, 128
+def known_buckets(length, buckets):
     positions = np.arange(length)
     offsets = positions[:, None] - positions[None, :]
     known = np.where(offsets < 0, buckets // 2, 0)
     for threshold in LIMITS:
         known = known + (np.abs(offsets) >= threshold)
+    return known
+
+
+def bias_of(bias_rows, length):
+    buckets, head_count = bias_rows.shape
+    high, wide = 8, 128
+    known = known_buckets(length, buckets)
+
+    def kernel(grid_ref, table_ref, bias_ref):
+        start = pl.program_id(0) * buckets
+        values = [table_ref[start + number] for number in range(buckets)]
+        for top in range(0, length, high):
+            for left in range(0, length, wide):
+                block = (slice(top, top + high), slice(left, left + wide))
+                first, *others = np.unique(known[block]).tolist()
+                bias = jnp.full((high, wide), values[first], jnp.float32)
+                if others:
+                    named = grid_ref[block]
+                    for number in others:
+                        bias = jnp.where(named == number, values[number], bias)
+                bias_ref[(0,) + block] = bias
+
+    return pl.pallas_call(
+        kernel,
+        grid=(head_count,),
+        out_shape=jax.ShapeDtypeStruct((head_count, length, length), jnp.float32),
+        in_specs=[
+            pl.BlockSpec((length, length), lambda h: (0, 0)),
+            pl.BlockSpec(memory_space=pltpu.SMEM),
+        ],
+        out_specs=pl.BlockSpec((1, length, length), lambda h: (h, 0, 0)),
+        compiler_params=pltpu.CompilerParams(vmem_limit_bytes=16 * 1024 * 1024),
+        cost_estimate=pl.CostEstimate(
+            flops=20 * head_count * length * length,
+            bytes_accessed=4 * head_count * length * length,
+            transcendentals=0,
+        ),
+    )(bucket_grid(length, buckets), bias_rows.T.reshape(-1))
+
+
+def bucket_sums(grid_grads, buckets):
+    head_count, length, _ = grid_grads.shape
+    high, wide = 8, 128
+    known = known_buckets(length, buckets)
 
     def kernel(grid_ref, grads_ref, table_ref):
         sums = [None] * buckets
@@ -115,14 +148,15 @@
     ]
 
 
-def sum_shards(near, far):
+def pass_on(near, far):
     wide = jnp.float32
     passed = (far[0].astype(wide) + from_partner(far[1], 1).astype(wide)).astype(jnp.bfloat16)
-    return (
-        near[0].astype(wide)
-        + from_partner(near[1], 1).astype(wide)
-        + from_partner(passed, 2).astype(wide)
-    )
+    return (near[0], from_partner(near[1], 1), passed)
+
+
+def add_shards(own, crossed, arrived):
+    wide = jnp.float32
+    return own.astype(wide) + crossed.astype(wide) + arrived.astype(wide)
 
 
 def to_owners(outgoing, local_experts):
@@ -368,20 +402,29 @@
     return jnp.einsum("sd,se->de", operands, grads, preferred_element_type=jnp.float32)
 
 
-def reduce_mixer(rows, sums, buckets):
+def reduce_mixer(rows, sums, buckets, expert_pairs):
     project = weight_grad(rows["normed"], rows["grad_projected"])
     output = weight_grad(rows["attended"], rows["grad_branch"])
     router = weight_grad(rows["routed"], rows["grad_logits"])
     table = bucket_sums(sums["grad_scores"], buckets)
     small = pack_small([router, sums["gains"]], table)
     packed = jnp.concatenate([project, output, small], axis=1).astype(jnp.bfloat16)
-    total = lax.psum(scatter_sum(packed, 0), "expert").astype(jnp.float32)
+    (own_in, crossed_in, passed_in), (own_out, crossed_out, passed_out) = expert_pairs
+    packed, arrived_out = lax.optimization_barrier((packed, from_partner(passed_out, 2)))
+    scattered = scatter_sum(packed, 0)
+    scattered, passed_in = lax.optimization_barrier((scattered, passed_in))
+    arrived_in = from_partner(passed_in, 2)
+    total = lax.psum(scattered, "expert").astype(jnp.float32)
+    expert_sum = (
+        add_shards(own_in, crossed_in, arrived_in),
+        add_shards(own_out, crossed_out, arrived_out),
+    )
     width = total.shape[0] * lax.axis_size("dp")
     query, key, value, output = (total[:, i * width : (i + 1) * width] for i in range(4))
     router, gains, table = unpack_small(
         total[:, 4 * width :], [router.shape[1], 2], table.shape, 1
     )
-    return (gains[:, 0], gains[:, 1], query, key, value, output, router, table)
+    return (gains[:, 0], gains[:, 1], query, key, value, output, router, table), expert_sum
 
 
 def pack_small(columns, table, shards=None):
@@ -429,7 +472,7 @@
     packed = jnp.concatenate([w_query[0], w_key[0], w_value[0], w_output[0], small], axis=1)
     packed = lax.all_gather(packed, "dp", axis=0, tiled=True)
     far_in = from_partner(expert_in[0], 2)
-    far_in, near_out = lax.optimization_barrier((far_in, expert_out[0]))
+    packed, near_out = lax.optimization_barrier((packed, expert_out[0]))
     far_out = from_partner(near_out, 2)
     w_in_use = gather_shards(expert_in[0], far_in)
     w_out_use = gather_shards(expert_out[0], far_out)
@@ -493,9 +536,10 @@
             for operand, grads in (("activated", "grad_rows"), ("grad_before", "grouped"))
             for first in (2, 0)
         ]
-        returned, halves = lax.optimization_barrier((returned, halves))
         far_out, near_out, far_in, near_in = halves
-        expert_sum.extend([sum_shards(near_in, far_in), sum_shards(near_out, far_out)])
+        pairs = (pass_on(near_in, far_in), pass_on(near_out, far_out))
+        returned, pairs = lax.optimization_barrier((returned, pairs))
+        expert_sum.extend(pairs)
         return returned
 
     for step_number in range(MICRO + 1):
@@ -528,7 +572,7 @@
         for name in mixer_kept[0]
         if name not in summed
     }
-    mixer_sum = reduce_mixer(rows, sums, buckets)
+    mixer_sum, expert_sum = reduce_mixer(rows, sums, buckets, expert_sum)
     pieces = [
         jnp.where(is_first, input_grads[micro_index], results[micro_index + 1])
         for micro_index in range(MICRO)

time: 880 us -> 870 us (0.989)
  other arithmetic: 109 us -> 60.7 us
  waiting for transfers between devices: 365 us -> 410 us
    psum x1, waiting for transfers between devices: 0.01 us -> 51.5 us  [reduce_mixer(): total = lax.psum(scattered, 'expert').astype(jnp.float32)]
    eq x31 -> x0, other arithmetic: 25 us -> none  [bias_of(): grid_values == number]
    ppermute x12, waiting for transfers between devices: 161 us -> 144 us  [from_partner(): lax.ppermute(block, 'dp', [(i, i ^ bit) for i in range(lax.axis_size('dp'...]
    all_to_all x4, waiting for transfers between devices: 41.7 us -> 58.8 us  [to_owners(): lax.all_to_all(outgoing.reshape(owners, local_experts, capacity, model_wi...]
    reduce_scatter x1, waiting for transfers between devices: 61.6 us -> 47.5 us  [scatter_sum(): return lax.psum_scatter(full, 'dp', scatter_dimension=axis, tiled=True)]
    select_n x1 -> x0, other arithmetic: 13.1 us -> none  [bias_of(): jnp.where(grid_values == number, bias_rows[number][:, None, None], bias)]
    unnamed x407 -> x307, local copies, waits for them, and re-layouts: 20.3 us -> 17.2 us
  transfers between devices with their start and end apart: 29 -> 29, of which waited for: 21 -> 19; matrix products, arithmetic and copies ran while one was open for 19% -> 15% of each run, Pallas kernels for 0% -> 1%
where the time goes in v3:
time: 870 us; the launch traced here: 859 us
  waiting for transfers between devices  410 us (47%)
  matrix products  201 us (23%)
  starting transfers between devices  60.8 us (7%)
  other arithmetic  60.7 us (7%)
  local copies, waits for them, and re-layouts  57.6 us (7%)
  blocking collectives  43 us (5%)
  between operations  16.7 us (2%)
  Pallas kernels  8.89 us (1%)
    ppermute x12, waiting for transfers between devices, from_partner(): lax.ppermute(block, 'dp', [(i, i ^ bit) for i in range(lax.axis_size('dp'...  144 us
    all_to_all x6, waiting for transfers between devices, to_tokens(): lax.all_to_all(produced.reshape(local_experts, owners, capacity, model_wi...  76.4 us
    all_to_all x4, waiting for transfers between devices, to_owners(): lax.all_to_all(outgoing.reshape(owners, local_experts, capacity, model_wi...  58.8 us
    psum x1, waiting for transfers between devices, reduce_mixer(): total = lax.psum(scattered, 'expert').astype(jnp.float32)  51.5 us
    reduce_scatter x1, waiting for transfers between devices, scatter_sum(): return lax.psum_scatter(full, 'dp', scatter_dimension=axis, tiled=True)  47.5 us
    all_to_all x2, blocking collectives, to_owners(): lax.all_to_all(outgoing.reshape(owners, local_experts, capacity, model_wi...  43 us
    dot_general x3, matrix products, expert_backward(): jnp.einsum('erd,efd->erf', grad_rows, w_out_use, preferred_element_type=j...  33.6 us
    ppermute x4, waiting for transfers between devices, from_behind(): return lax.ppermute(block, axis, route)  32.4 us
  transfers between devices with their start and end apart: 29, of which 19 were waited for; matrix products, arithmetic and copies ran while one was open for 15% of the time, Pallas kernels for 1%

profile of v3, /device:TPU:0, one launch (start us, length us, event | category | flops | bytes accessed | tf_op | source)
XLA Modules:
  0.0 859.3 jit_solution(9254022746105069050)
XLA Ops:
  18.2 76.7 %collective-permute-done.1 = bf16[2,768,768]{2,1,0:T(8,128)(2,1)} collective-permute-done((bf16[2,768,768]{2,1,0:T(8,128)(2,1)}, bf16[2,768,768]{2,1,0:T(8,128)(2,1)}, u32[]{:S(2)}, u32[]{:S(2)}) %collective-permute-start.1) | collective-permute-done | bytes 2359328 | tf_op jit(solution)/shard_map/ppermute | solution.py:131
  113.9 37.6 %collective-permute-done.4 = bf16[2,768,768]{2,1,0:T(8,128)(2,1)} collective-permute-done((bf16[2,768,768]{2,1,0:T(8,128)(2,1)}, bf16[2,768,768]{2,1,0:T(8,128)(2,1)}, u32[]{:S(2)}, u32[]{:S(2)}) %collective-permute-start.4) | collective-permute-done | bytes 2359328 | tf_op jit(solution)/shard_map/ppermute | solution.py:131
  158.7 8.7 %pad_maximum_fusion = bf16[2,3072,768]{2,1,0:T(8,128)(2,1)} fusion(bf16[2,768,768]{2,1,0:T(8,128)(2,1)} %collective-permute-done.2, bf16[2,768,768]{2,1,0:T(8,128)(2,1)} %collective-permute-done.1, bf16[2,768,768]{2,1,0:T(8,128)(2,1)} %collective-permute-done, bf16[2,768,768]{2,1,0:T(8,128)(2,1)} %bitcast.24), kind=kLoop, calls=%fused_computation | loop fusion | flops 37748736 | bytes 18874368 | tf_op jit(solution)/shard_map/concatenate | solution.py:135
  167.4 12.2 %all-to-all-done = bf16[4,2,64,768]{3,2,1,0:T(8,128)(2,1)} async-done(((bf16[4,2,64,768]{3,2,1,0:T(8,128)(2,1)}), bf16[4,2,64,768]{3,2,1,0:T(8,128)(2,1)}, u32[]{:S(2)}, u32[]{:S(2)}) %all-to-all-start) | async-done | bytes 786464 | tf_op jit(solution)/shard_map/all_to_all | solution.py:166
  180.8 5.5 fusion.249
  186.4 6.8 pad_maximum_fusion.1
  203.7 18.6 %all-to-all-done.1 = bf16[4,2,64,768]{3,2,1,0:T(8,128)(2,1)} async-done(((bf16[4,2,64,768]{3,2,1,0:T(8,128)(2,1)}), bf16[4,2,64,768]{3,2,1,0:T(8,128)(2,1)}, u32[]{:S(2)}, u32[]{:S(2)}) %all-to-all-start.1) | async-done | bytes 786464 | tf_op jit(solution)/shard_map/all_to_all | solution.py:180
  228.7 7.3 collective-permute-done.6
  255.4 21.1 %all_to_all.60 = bf16[4,2,64,768]{3,2,1,0:T(8,128)(2,1)S(1)} all-to-all(bf16[4,2,64,768]{3,2,1,0:T(8,128)(2,1)S(1)} %bitcast.333), channel_id=1, replica_groups=mesh['section'=2,'expert'=4,'dp'=4] {'expert'}, dimensions={0} | all-to-all | bytes 1572864 | tf_op jit(solution)/shard_map/all_to_all | solution.py:166
  281.8 7.5 convolution_convert_fusion.19
  295.8 17.7 %all-to-all-done.3 = bf16[4,2,64,768]{3,2,1,0:T(8,128)(2,1)} async-done(((bf16[4,2,64,768]{3,2,1,0:T(8,128)(2,1)}), bf16[4,2,64,768]{3,2,1,0:T(8,128)(2,1)}, u32[]{:S(2)}, u32[]{:S(2)}) %all-to-all-start.3) | async-done | bytes 786464 | tf_op jit(solution)/shard_map/all_to_all | solution.py:180
  320.7 7.4 collective-permute-done.7
  355.3 16.0 %all-to-all-done.5 = bf16[4,2,64,768]{3,2,1,0:T(8,128)(2,1)S(1)} async-done(((bf16[4,2,64,768]{3,2,1,0:T(8,128)(2,1)}), bf16[4,2,64,768]{3,2,1,0:T(8,128)(2,1)S(1)}, u32[]{:S(2)}, u32[]{:S(2)}) %all-to-all-start.5) | async-done | bytes 786464 | tf_op jit(solution)/shard_map/all_to_all | solution.py:166
  375.6 19.6 %all-to-all-done.4 = bf16[4,2,64,768]{3,2,1,0:T(8,128)(2,1)} async-done(((bf16[4,2,64,768]{3,2,1,0:T(8,128)(2,1)}), bf16[4,2,64,768]{3,2,1,0:T(8,128)(2,1)}, u32[]{:S(2)}, u32[]{:S(2)}) %all-to-all-start.4) | async-done | bytes 786464 | tf_op jit(solution)/shard_map/all_to_all | solution.py:166
  396.4 5.5 fusion.250
  401.9 9.1 %convolution_convert_fusion.15 = bf16[2,256,768]{2,1,0:T(8,128)(2,1)S(1)} fusion(bf16[2,3072,768]{2,1,0:T(8,128)(2,1)} %copy-done.47, f32[2,256,3072]{2,1,0:T(8,128)S(1)} %fusion.250), kind=kOutput, calls=%fused_computation.129 | convolution fusion | flops 2430468096 | bytes 16515072 | tf_op jit(solution)/shard_map/erf,efd->erd/dot_general | solution.py:193
  415.7 8.7 %fusion.20 = bf16[2,256,3072]{2,1,0:T(8,128)(2,1)S(1)} fusion(f32[2,256,3072]{2,1,0:T(8,128)} %copy-done.59, bf16[2,256,768]{2,1,0:T(8,128)(2,1)S(1)} %bitcast.300, bf16[2,3072,768]{2,1,0:T(8,128)(2,1)} %copy-done.47), kind=kOutput, calls=%fused_computation.40 | convolution fusion | flops 2447376384 | bytes 19660800 | tf_op jit(solution)/shard_map/erd,efd->erf/dot_general | solution.py:198
  424.4 7.5 convolution_convert_fusion.16
  443.4 15.8 %all-to-all-done.6 = bf16[4,2,64,768]{3,2,1,0:T(8,128)(2,1)S(1)} async-done(((bf16[4,2,64,768]{3,2,1,0:T(8,128)(2,1)}), bf16[4,2,64,768]{3,2,1,0:T(8,128)(2,1)S(1)}, u32[]{:S(2)}, u32[]{:S(2)}) %all-to-all-start.6) | async-done | bytes 786464 | tf_op jit(solution)/shard_map/all_to_all | solution.py:180
  476.2 10.8 %collective-permute-done.8 = bf16[256,768]{1,0:T(8,128)(2,1)S(1)} collective-permute-done((bf16[256,768]{1,0:T(8,128)(2,1)S(1)}, bf16[256,768]{1,0:T(8,128)(2,1)S(1)}, u32[]{:S(2)}, u32[]{:S(2)}) %collective-permute-start.8) | collective-permute-done | bytes 393248 | tf_op jit(solution)/shard_map/ppermute | solution.py:20
  487.5 21.9 %all_to_all.61 = bf16[4,2,64,768]{3,2,1,0:T(8,128)(2,1)S(1)} all-to-all(bf16[4,2,64,768]{3,2,1,0:T(8,128)(2,1)S(1)} %bitcast.337), channel_id=1, replica_groups=mesh['section'=2,'expert'=4,'dp'=4] {'expert'}, dimensions={0} | all-to-all | bytes 1572864 | tf_op jit(solution)/shard_map/all_to_all | solution.py:166
  509.5 8.1 fusion.13
  525.8 18.8 %all-to-all-done.9 = bf16[4,2,64,768]{3,2,1,0:T(8,128)(2,1)} async-done(((bf16[4,2,64,768]{3,2,1,0:T(8,128)(2,1)}), bf16[4,2,64,768]{3,2,1,0:T(8,128)(2,1)}, u32[]{:S(2)}, u32[]{:S(2)}) %all-to-all-start.9) | async-done | bytes 786464 | tf_op jit(solution)/shard_map/all_to_all | solution.py:180
  570.1 7.0 collective-permute-done.9
  590.6 11.0 %all-to-all-done.10 = bf16[4,2,64,768]{3,2,1,0:T(8,128)(2,1)} async-done(((bf16[4,2,64,768]{3,2,1,0:T(8,128)(2,1)}), bf16[4,2,64,768]{3,2,1,0:T(8,128)(2,1)}, u32[]{:S(2)}, u32[]{:S(2)}) %all-to-all-start.10) | async-done | bytes 786464 | tf_op jit(solution)/shard_map/all_to_all | solution.py:166
  603.8 16.8 %broadcast_select_fusion.1 = (bf16[2,256,3072]{2,1,0:T(8,128)(2,1)S(1)}, bf16[2,256,3072]{2,1,0:T(8,128)(2,1)}, bf16[2,256,3072]{2,1,0:T(8,128)(2,1)}) fusion(bf16[2,256,3072]{2,1,0:T(8,128)(2,1)} %copy-done.131, pred[]{:T(512)S(6)} %eq.59, f32[2,256,3072]{2,1,0:T(8,128)} %copy-done.58, f32[2,256,3072]{2,1,0:T(8,128)} %copy-done.59, ...), kind=kOutput, calls=%fused_computation.70 | convolution fusion | flops 2467823616 | bytes 35389440 | tf_op jit(solution)/shard_map/erd,efd->erf/dot_general | solution.py:198
  620.7 5.5 convolution_convert_fusion.4
  694.8 7.2 convolution_convert_fusion
  704.5 29.4 %collective-permute-done.14 = bf16[2,768,768]{2,1,0:T(8,128)(2,1)} collective-permute-done((bf16[2,768,768]{2,1,0:T(8,128)(2,1)}, bf16[2,768,768]{2,1,0:T(8,128)(2,1)}, u32[]{:S(2)}, u32[]{:S(2)}) %collective-permute-start.14) | collective-permute-done | bytes 2359328 | tf_op jit(solution)/shard_map/ppermute | solution.py:131
  734.0 47.5 %reduce-scatter.2.cloned.1.call-done = bf16[192,3200]{1,0:T(8,128)(2,1)} async-done(((bf16[768,3200]{1,0:T(8,128)(2,1)}), bf16[192,3200]{1,0:T(8,128)(2,1)}) %reduce-scatter.2.cloned.1.call-update) | async-done | bytes 1228816 | tf_op jit(solution)/shard_map/reduce_scatter | solution.py:398
  790.2 51.5 %all-reduce.6.cloned.1.call-done = bf16[192,3200]{1,0:T(8,128)(2,1)} async-done(((bf16[192,3200]{1,0:T(8,128)(2,1)}), bf16[192,3200]{1,0:T(8,128)(2,1)}) %all-reduce.6.cloned.1.call-update) | async-done | bytes 1228816 | tf_op jit(solution)/shard_map/psum | solution.py:417
  846.8 5.5 add_bitcast_fusion.1
  (544 shorter events, 292.4 us)
Async XLA Ops:
  7.2 87.7 %all-gather.2.cloned.1.call-start = ((), (), s32[]{:S(2)}) async-start(), calls=%async_computation.13 | async-start | bytes 6144000 | tf_op jit(solution)/shard_map/all_gather | solution.py:473
  14.0 80.9 %collective-permute-start.1 = (bf16[2,768,768]{2,1,0:T(8,128)(2,1)}, bf16[2,768,768]{2,1,0:T(8,128)(2,1)}, u32[]{:S(2)}, u32[]{:S(2)}) collective-permute-start(bf16[2,768,768]{2,1,0:T(8,128)(2,1)} %bitcast.24), channel_id=1, source_target_pairs={{0,2},{1,3},{2,0},{3,1},{4,6},{5,7},{6,4},{7,5},{8,10},{9,11},{10,... | collective-permute-start | bytes 7077896 | tf_op jit(solution)/shard_map/ppermute | solution.py:131
  17.0 141.7 %collective-permute-start = (bf16[2,768,768]{2,1,0:T(8,128)(2,1)}, bf16[2,768,768]{2,1,0:T(8,128)(2,1)}, u32[]{:S(2)}, u32[]{:S(2)}) collective-permute-start(bf16[2,768,768]{2,1,0:T(8,128)(2,1)} %bitcast.24), channel_id=1, source_target_pairs={{0,1},{1,0},{2,3},{3,2},{4,5},{5,4},{6,7},{7,6},{8,9},{9,8},{10,11... | collective-permute-start | bytes 7077896 | tf_op jit(solution)/shard_map/ppermute | solution.py:131
  17.0 169.4 %collective-permute-start.3 = (bf16[2,768,768]{2,1,0:T(8,128)(2,1)}, bf16[2,768,768]{2,1,0:T(8,128)(2,1)}, u32[]{:S(2)}, u32[]{:S(2)}) collective-permute-start(bf16[2,768,768]{2,1,0:T(8,128)(2,1)} %bitcast.11), channel_id=1, source_target_pairs={{0,1},{1,0},{2,3},{3,2},{4,5},{5,4},{6,7},{7,6},{8,9},{9,8},{10,11... | collective-permute-start | bytes 7077896 | tf_op jit(solution)/shard_map/ppermute | solution.py:131
  18.2 84.2 %copy-start.128 = (f32[256]{0:T(256)}, f32[256]{0:T(256)S(1)}, u32[]{:S(2)}) copy-start(f32[256]{0:T(256)S(1)} %add_rsqrt_fusion.5) | copy-start | bytes 3076
  94.9 63.8 %collective-permute-start.2 = (bf16[2,768,768]{2,1,0:T(8,128)(2,1)}, bf16[2,768,768]{2,1,0:T(8,128)(2,1)}, u32[]{:S(2)}, u32[]{:S(2)}) collective-permute-start(bf16[2,768,768]{2,1,0:T(8,128)(2,1)} %collective-permute-done.1), channel_id=1, source_target_pairs={{0,1},{1,0},{2,3},{3,2},{4,5},{5,4},{6,7},{7,6},{8,9},{9,8},{10,11... | collective-permute-start | bytes 7077896 | tf_op jit(solution)/shard_map/ppermute | solution.py:131
  97.5 54.0 %collective-permute-start.4 = (bf16[2,768,768]{2,1,0:T(8,128)(2,1)}, bf16[2,768,768]{2,1,0:T(8,128)(2,1)}, u32[]{:S(2)}, u32[]{:S(2)}) collective-permute-start(bf16[2,768,768]{2,1,0:T(8,128)(2,1)} %bitcast.11), channel_id=1, source_target_pairs={{0,2},{1,3},{2,0},{3,1},{4,6},{5,7},{6,4},{7,5},{8,10},{9,11},{10,... | collective-permute-start | bytes 7077896 | tf_op jit(solution)/shard_map/ppermute | solution.py:131
  113.9 233.1 %copy-start.126 = (f32[256]{0:T(256)}, f32[256]{0:T(256)S(1)}, u32[]{:S(2)}) copy-start(f32[256]{0:T(256)S(1)} %add_rsqrt_fusion.4) | copy-start | bytes 3076
  151.5 34.9 %collective-permute-start.5 = (bf16[2,768,768]{2,1,0:T(8,128)(2,1)}, bf16[2,768,768]{2,1,0:T(8,128)(2,1)}, u32[]{:S(2)}, u32[]{:S(2)}) collective-permute-start(bf16[2,768,768]{2,1,0:T(8,128)(2,1)} %collective-permute-done.4), channel_id=1, source_target_pairs={{0,1},{1,0},{2,3},{3,2},{4,5},{5,4},{6,7},{7,6},{8,9},{9,8},{10,11... | collective-permute-start | bytes 7077896 | tf_op jit(solution)/shard_map/ppermute | solution.py:131
  153.7 26.0 %all-to-all-start = ((bf16[4,2,64,768]{3,2,1,0:T(8,128)(2,1)}), bf16[4,2,64,768]{3,2,1,0:T(8,128)(2,1)}, u32[]{:S(2)}, u32[]{:S(2)}) async-start(bf16[4,2,64,768]{3,2,1,0:T(8,128)(2,1)} %bitcast.309), calls=%async_computation | async-start | bytes 1572864 | tf_op jit(solution)/shard_map/all_to_all | solution.py:166
  197.7 24.7 %all-to-all-start.1 = ((bf16[4,2,64,768]{3,2,1,0:T(8,128)(2,1)}), bf16[4,2,64,768]{3,2,1,0:T(8,128)(2,1)}, u32[]{:S(2)}, u32[]{:S(2)}) async-start(bf16[4,2,64,768]{3,2,1,0:T(8,128)(2,1)} %bitcast.304), calls=%async_computation.1 | async-start | bytes 1572864 | tf_op jit(solution)/shard_map/all_to_all | solution.py:180
  225.0 11.0 %collective-permute-start.6 = (bf16[256,768]{1,0:T(8,128)(2,1)S(1)}, bf16[256,768]{1,0:T(8,128)(2,1)S(1)}, u32[]{:S(2)}, u32[]{:S(2)}) collective-permute-start(bf16[256,768]{1,0:T(8,128)(2,1)S(1)} %get-tuple-element.170), channel_id=1, source_target_pairs={{0,16},{1,17},{2,18},{3,19},{4,20},{5,21},{6,22},{7,23},{8,24},{9,... | collective-permute-start | bytes 1179656 | tf_op jit(solution)/shard_map/ppermute | solution.py:20
  290.2 23.2 %all-to-all-start.3 = ((bf16[4,2,64,768]{3,2,1,0:T(8,128)(2,1)}), bf16[4,2,64,768]{3,2,1,0:T(8,128)(2,1)}, u32[]{:S(2)}, u32[]{:S(2)}) async-start(bf16[4,2,64,768]{3,2,1,0:T(8,128)(2,1)} %bitcast.305), calls=%async_computation.3 | async-start | bytes 1572864 | tf_op jit(solution)/shard_map/all_to_all | solution.py:180
  316.1 11.9 %collective-permute-start.7 = (bf16[256,768]{1,0:T(8,128)(2,1)S(1)}, bf16[256,768]{1,0:T(8,128)(2,1)S(1)}, u32[]{:S(2)}, u32[]{:S(2)}) collective-permute-start(bf16[256,768]{1,0:T(8,128)(2,1)S(1)} %get-tuple-element.180), channel_id=1, source_target_pairs={{0,16},{1,17},{2,18},{3,19},{4,20},{5,21},{6,22},{7,23},{8,24},{9,... | collective-permute-start | bytes 1179656 | tf_op jit(solution)/shard_map/ppermute | solution.py:20
  346.9 112.3 %copy-start.45 = (f32[256,768]{1,0:T(8,128)}, f32[256,768]{1,0:T(8,128)S(1)}, u32[]{:S(2)}) copy-start(f32[256,768]{1,0:T(8,128)S(1)} %get-tuple-element.185) | copy-start | bytes 2359300
  349.2 22.1 %all-to-all-start.5 = ((bf16[4,2,64,768]{3,2,1,0:T(8,128)(2,1)}), bf16[4,2,64,768]{3,2,1,0:T(8,128)(2,1)S(1)}, u32[]{:S(2)}, u32[]{:S(2)}) async-start(bf16[4,2,64,768]{3,2,1,0:T(8,128)(2,1)} %bitcast.310), calls=%async_computation.5 | async-start | bytes 1572864 | tf_op jit(solution)/shard_map/all_to_all | solution.py:166
  371.4 23.9 %all-to-all-start.4 = ((bf16[4,2,64,768]{3,2,1,0:T(8,128)(2,1)}), bf16[4,2,64,768]{3,2,1,0:T(8,128)(2,1)}, u32[]{:S(2)}, u32[]{:S(2)}) async-start(bf16[4,2,64,768]{3,2,1,0:T(8,128)(2,1)} %bitcast.45), calls=%async_computation.4 | async-start | bytes 1572864 | tf_op jit(solution)/shard_map/all_to_all | solution.py:166
  412.0 23.3 %all-to-all-start.7 = ((bf16[4,2,64,768]{3,2,1,0:T(8,128)(2,1)}), bf16[4,2,64,768]{3,2,1,0:T(8,128)(2,1)S(1)}, u32[]{:S(2)}, u32[]{:S(2)}) async-start(bf16[4,2,64,768]{3,2,1,0:T(8,128)(2,1)} %bitcast.248), calls=%async_computation.7 | async-start | bytes 1572864 | tf_op jit(solution)/shard_map/all_to_all | solution.py:180
  436.2 23.1 %all-to-all-start.6 = ((bf16[4,2,64,768]{3,2,1,0:T(8,128)(2,1)}), bf16[4,2,64,768]{3,2,1,0:T(8,128)(2,1)S(1)}, u32[]{:S(2)}, u32[]{:S(2)}) async-start(bf16[4,2,64,768]{3,2,1,0:T(8,128)(2,1)} %bitcast.249), calls=%async_computation.6 | async-start | bytes 1572864 | tf_op jit(solution)/shard_map/all_to_all | solution.py:180
  474.9 12.1 %collective-permute-start.8 = (bf16[256,768]{1,0:T(8,128)(2,1)S(1)}, bf16[256,768]{1,0:T(8,128)(2,1)S(1)}, u32[]{:S(2)}, u32[]{:S(2)}) collective-permute-start(bf16[256,768]{1,0:T(8,128)(2,1)S(1)} %fusion.84), channel_id=1, source_target_pairs={{16,0},{17,1},{18,2},{19,3},{20,4},{21,5},{22,6},{23,7},{24,8},{25... | collective-permute-start | bytes 1179656 | tf_op jit(solution)/shard_map/ppermute | solution.py:20
  521.3 23.3 %all-to-all-start.9 = ((bf16[4,2,64,768]{3,2,1,0:T(8,128)(2,1)}), bf16[4,2,64,768]{3,2,1,0:T(8,128)(2,1)}, u32[]{:S(2)}, u32[]{:S(2)}) async-start(bf16[4,2,64,768]{3,2,1,0:T(8,128)(2,1)} %bitcast.247), calls=%async_computation.9 | async-start | bytes 1572864 | tf_op jit(solution)/shard_map/all_to_all | solution.py:180
  564.8 12.3 %collective-permute-start.9 = (bf16[256,768]{1,0:T(8,128)(2,1)}, bf16[256,768]{1,0:T(8,128)(2,1)S(1)}, u32[]{:S(2)}, u32[]{:S(2)}) collective-permute-start(bf16[256,768]{1,0:T(8,128)(2,1)} %get-tuple-element.151), channel_id=1, source_target_pairs={{16,0},{17,1},{18,2},{19,3},{20,4},{21,5},{22,6},{23,7},{24,8},{25... | collective-permute-start | bytes 1179656 | tf_op jit(solution)/shard_map/ppermute | solution.py:20
  578.5 23.1 %all-to-all-start.10 = ((bf16[4,2,64,768]{3,2,1,0:T(8,128)(2,1)}), bf16[4,2,64,768]{3,2,1,0:T(8,128)(2,1)}, u32[]{:S(2)}, u32[]{:S(2)}) async-start(bf16[4,2,64,768]{3,2,1,0:T(8,128)(2,1)} %bitcast.329), calls=%async_computation.10 | async-start | bytes 1572864 | tf_op jit(solution)/shard_map/all_to_all | solution.py:166
  626.2 27.9 %collective-permute-start.13 = (bf16[2,768,768]{2,1,0:T(8,128)(2,1)}, bf16[2,768,768]{2,1,0:T(8,128)(2,1)}, u32[]{:S(2)}, u32[]{:S(2)}) collective-permute-start(bf16[2,768,768]{2,1,0:T(8,128)(2,1)} %convolution_convert_fusion.4), channel_id=1, source_target_pairs={{0,1},{1,0},{2,3},{3,2},{4,5},{5,4},{6,7},{7,6},{8,9},{9,8},{10,11... | collective-permute-start | bytes 7077896 | tf_op jit(solution)/shard_map/ppermute | solution.py:131
  631.2 27.5 %collective-permute-start.11 = (bf16[2,768,768]{2,1,0:T(8,128)(2,1)}, bf16[2,768,768]{2,1,0:T(8,128)(2,1)}, u32[]{:S(2)}, u32[]{:S(2)}) collective-permute-start(bf16[2,768,768]{2,1,0:T(8,128)(2,1)} %convolution_convert_fusion.7), channel_id=1, source_target_pairs={{0,1},{1,0},{2,3},{3,2},{4,5},{5,4},{6,7},{7,6},{8,9},{9,8},{10,11... | collective-permute-start | bytes 7077896 | tf_op jit(solution)/shard_map/ppermute | solution.py:131
  634.7 31.9 %collective-permute-start.12 = (bf16[2,768,768]{2,1,0:T(8,128)(2,1)}, bf16[2,768,768]{2,1,0:T(8,128)(2,1)}, u32[]{:S(2)}, u32[]{:S(2)}) collective-permute-start(bf16[2,768,768]{2,1,0:T(8,128)(2,1)} %convolution_convert_fusion.5), channel_id=1, source_target_pairs={{0,1},{1,0},{2,3},{3,2},{4,5},{5,4},{6,7},{7,6},{8,9},{9,8},{10,11... | collective-permute-start | bytes 7077896 | tf_op jit(solution)/shard_map/ppermute | solution.py:131
  637.6 29.0 %collective-permute-start.10 = (bf16[2,768,768]{2,1,0:T(8,128)(2,1)}, bf16[2,768,768]{2,1,0:T(8,128)(2,1)}, u32[]{:S(2)}, u32[]{:S(2)}) collective-permute-start(bf16[2,768,768]{2,1,0:T(8,128)(2,1)} %convolution_convert_fusion.8), channel_id=1, source_target_pairs={{0,1},{1,0},{2,3},{3,2},{4,5},{5,4},{6,7},{7,6},{8,9},{9,8},{10,11... | collective-permute-start | bytes 7077896 | tf_op jit(solution)/shard_map/ppermute | solution.py:131
  641.7 24.8 %all-to-all-start.11 = ((bf16[4,2,64,768]{3,2,1,0:T(8,128)(2,1)}), bf16[4,2,64,768]{3,2,1,0:T(8,128)(2,1)}, u32[]{:S(2)}, u32[]{:S(2)}) async-start(bf16[4,2,64,768]{3,2,1,0:T(8,128)(2,1)} %bitcast.302), calls=%async_computation.11 | async-start | bytes 1572864 | tf_op jit(solution)/shard_map/all_to_all | solution.py:180
  645.9 135.6 %reduce-scatter.2.cloned.1.call-start = ((), (), s32[]{:S(2)}) async-start(), calls=%async_computation.14 | async-start | bytes 6144000 | tf_op jit(solution)/shard_map/reduce_scatter | solution.py:398
  681.2 52.7 %collective-permute-start.14 = (bf16[2,768,768]{2,1,0:T(8,128)(2,1)}, bf16[2,768,768]{2,1,0:T(8,128)(2,1)}, u32[]{:S(2)}, u32[]{:S(2)}) collective-permute-start(bf16[2,768,768]{2,1,0:T(8,128)(2,1)} %add_convert_fusion), channel_id=1, source_target_pairs={{0,2},{1,3},{2,0},{3,1},{4,6},{5,7},{6,4},{7,5},{8,10},{9,11},{10,... | collective-permute-start | bytes 7077896 | tf_op jit(solution)/shard_map/ppermute | solution.py:131
  733.9 107.8 %all-reduce.6.cloned.1.call-start = ((), (), s32[]{:S(2)}) async-start(), calls=%async_computation.15 | async-start | bytes 2457600 | tf_op jit(solution)/shard_map/psum | solution.py:417
  781.5 65.4 %collective-permute-start.15 = (bf16[2,768,768]{2,1,0:T(8,128)(2,1)}, bf16[2,768,768]{2,1,0:T(8,128)(2,1)}, u32[]{:S(2)}, u32[]{:S(2)}) collective-permute-start(bf16[2,768,768]{2,1,0:T(8,128)(2,1)} %add_convert_fusion.1), channel_id=1, source_target_pairs={{0,2},{1,3},{2,0},{3,1},{4,6},{5,7},{6,4},{7,5},{8,10},{9,11},{10,... | collective-permute-start | bytes 7077896 | tf_op jit(solution)/shard_map/ppermute | solution.py:131
  (147 other events, 1284.8 us)
Sparse Core Ops, SparseCore 0:
  14.1 67.7 all-gather.1
  734.0 47.3 reduce-scatter.1
  784.0 57.7 all-reduce.5
